TPU v7x, 32 devices: a whole 2x2x4 slice. The times are simulated.
32 devices in a mesh: band: 4 (over y, x), lon: 8 (over z, core).
Axes of the slice: x: 2, y: 2, z: 4, core: 2. Of those that a mesh axis runs over, the one named last changes fastest.
Arguments:
- latent: bfloat16 [128, 1024, 256], P('band', 'lon'), may hold values from -6 to 6
- row_index: int32 [4, 8, 16], P('band', 'lon'), may hold values from 0 to 31
- interp_weights: bfloat16 [512, 128, 128], P(('band', 'lon')), may hold values from -0.5 to 0.5
- observation_slot_index: int32 [512, 128], P(('band', 'lon')), may hold values from 0 to 6
- counts: int32 [512], P(('band', 'lon')), may hold values from 32 to 128
- targets: bfloat16 [512, 128, 128], P(('band', 'lon')), may hold values from -6 to 6
- gain: float32 [256], replicated, may hold values from 0.5 to 1.5
- w_in: bfloat16 [256, 512], replicated, may hold values from -0.375 to 0.375
- w_out: bfloat16 [512, 256], replicated, may hold values from -0.25 to 0.25
- head: bfloat16 [256, 128], replicated, may hold values from -0.375 to 0.375
Outputs:
- grad_latent: float32 [128, 1024, 256], P('band', 'lon')
- grad_w_in: float32 [256, 512], replicated
- grad_w_out: float32 [512, 256], replicated
- grad_gain: float32 [256], replicated
- grad_head: float32 [256, 128], replicated
All inputs are finite; a program needn't handle non-finite values.
Results may differ from a plain program's by a relative error of at most 0.007.
Values may be sent and summed in bfloat16 or wider, within the bound.
A program may use at most 128 MiB of HBM per device.

v0:
```python
import math

import jax
import jax.numpy as jnp
from jax import lax
from jax.sharding import PartitionSpec as P

WINDOW_SLOTS = 7


norm_eps = 1e-05


def padded_2(cells, sides, width):
    for axis, dim in sides:
        count = lax.axis_size(axis)
        head = lax.slice_in_dim(cells, 0, width, axis=dim)
        tail = lax.slice_in_dim(cells, cells.shape[dim] - width, cells.shape[dim], axis=dim)
        cells = jnp.concatenate(
            [
                lax.ppermute(tail, axis, [(i, (i + 1) % count) for i in range(count)]),
                cells,
                lax.ppermute(head, axis, [((i + 1) % count, i) for i in range(count)]),
            ],
            axis=dim,
        )
    return cells


def rounded_slots(values):
    return lax.optimization_barrier(values.astype(jnp.bfloat16))


def padded_mix(padded):
    return padded[:, 1:-1] + 0.5 * (padded[:, :-2] + padded[:, 2:])


def silu_slope(pre_act):
    sigmoid_a = jax.nn.sigmoid(pre_act)
    return sigmoid_a * (1.0 + pre_act * (1.0 - sigmoid_a))


def project_pair(weights, tile_pairs, temporal_weight, channels):
    proj_old = jnp.einsum(
        "bol,blc->boc", weights, tile_pairs[..., :channels], preferred_element_type=jnp.float32
    )
    proj_new = jnp.einsum(
        "bol,blc->boc", weights, tile_pairs[..., channels:], preferred_element_type=jnp.float32
    )
    return ((1.0 - temporal_weight) * proj_old + temporal_weight * proj_new).astype(jnp.bfloat16)


def pull_back(weights, obs_grad, temporal_weight):
    obs_float = obs_grad.astype(jnp.float32)
    back_old = ((1.0 - temporal_weight) * obs_float).astype(jnp.bfloat16)
    back_new = (temporal_weight * obs_float).astype(jnp.bfloat16)
    tile_old = jnp.einsum("bol,boc->blc", weights, back_old, preferred_element_type=jnp.float32)
    tile_new = jnp.einsum("bol,boc->blc", weights, back_new, preferred_element_type=jnp.float32)
    return jnp.concatenate([tile_old, tile_new], axis=-1).astype(jnp.bfloat16)


def decode(obs_latent, live_rows, goals, head, loss_scale):
    blocks, obs_rows, channels = obs_latent.shape
    flat_latent = obs_latent.reshape(-1, channels)
    predicted = jnp.dot(flat_latent, head, preferred_element_type=jnp.float32)
    residual = jnp.where(
        live_rows, predicted - goals.reshape(-1, head.shape[1]).astype(jnp.float32), 0.0
    )
    pred_grad = (residual * loss_scale).astype(jnp.bfloat16)
    head_grad = jnp.einsum("rc,rv->cv", flat_latent, pred_grad, preferred_element_type=jnp.float32)
    obs_grad = jnp.einsum("rv,cv->rc", pred_grad, head, preferred_element_type=jnp.float32).astype(
        jnp.bfloat16
    )
    return (head_grad, obs_grad.reshape(blocks, obs_rows, channels))


def body(
    latent,
    row_index,
    interp_weights,
    observation_slot_index,
    counts,
    targets,
    gain,
    w_in,
    w_out,
    head,
):
    lat_rows, lon_cells, channels = latent.shape
    peer_count = lax.axis_size("lon")
    devices_all = lax.axis_size("band") * peer_count
    blocks = interp_weights.shape[0]
    obs_rows = interp_weights.shape[1]
    per_peer = blocks // peer_count
    padded = padded_2(latent, (("lon", 1),), 1)
    summed = padded_mix(padded.astype(jnp.float32))
    inv_rms = lax.rsqrt(jnp.mean(summed * summed, axis=-1, keepdims=True) + norm_eps)
    normed = (summed * inv_rms * gain).astype(jnp.bfloat16)
    pre_act = jnp.einsum("lmc,ch->lmh", normed, w_in, preferred_element_type=jnp.float32)
    activated = jax.nn.silu(pre_act).astype(jnp.bfloat16)
    advanced = (
        latent.astype(jnp.float32)
        + jnp.einsum("lmh,hc->lmc", activated, w_out, preferred_element_type=jnp.float32)
    ).astype(jnp.bfloat16)
    stacked = jnp.concatenate([latent, advanced], axis=-1)
    requested = row_index.reshape(blocks)
    picked = stacked[requested]
    row_select = (requested[:, None] == jnp.arange(lat_rows, dtype=jnp.int32)[None, :]).astype(
        jnp.bfloat16
    )
    temporal_weight = rounded_slots(observation_slot_index.astype(jnp.float32) / (WINDOW_SLOTS - 1))
    live_flags = jnp.arange(obs_rows, dtype=jnp.int32)[None, :] < counts[:, None]
    live_rows = live_flags.reshape(-1, 1)
    loss_scale = 1.0 / math.sqrt(obs_rows)
    tile_pairs = lax.all_to_all(
        picked.reshape(peer_count, per_peer, lon_cells, 2 * channels),
        "lon",
        split_axis=0,
        concat_axis=0,
        tiled=True,
    )
    local_coef = temporal_weight.reshape(blocks, obs_rows, 1).astype(jnp.float32)
    obs_latent = project_pair(
        interp_weights, tile_pairs.reshape(blocks, lon_cells, 2 * channels), local_coef, channels
    )
    head_grad, obs_grad = decode(obs_latent, live_rows, targets, head, loss_scale)
    tile_grads = pull_back(interp_weights, obs_grad, local_coef)
    returned = lax.all_to_all(
        tile_grads.reshape(peer_count, per_peer, lon_cells, 2 * channels),
        "lon",
        split_axis=0,
        concat_axis=0,
        tiled=True,
    )
    grid_grad = jnp.einsum(
        "br,bx->rx",
        row_select,
        returned.reshape(blocks, lon_cells * 2 * channels),
        preferred_element_type=jnp.float32,
    )
    grid_grad = grid_grad.reshape(lat_rows, lon_cells, 2 * channels)
    grad_adv = grid_grad[..., channels:].astype(jnp.bfloat16)
    grad_out = jnp.einsum("lmh,lmc->hc", activated, grad_adv, preferred_element_type=jnp.float32)
    act_grad = jnp.einsum("lmc,hc->lmh", grad_adv, w_out, preferred_element_type=jnp.float32)
    pre_grad = (act_grad * silu_slope(pre_act)).astype(jnp.bfloat16)
    grad_in = jnp.einsum("lmc,lmh->ch", normed, pre_grad, preferred_element_type=jnp.float32)
    normed_grad = jnp.einsum("lmh,ch->lmc", pre_grad, w_in, preferred_element_type=jnp.float32)
    grad_gain = jnp.sum(normed_grad * summed * inv_rms, axis=(0, 1))
    gained = normed_grad * gain
    summed_grad = inv_rms * (
        gained - summed * inv_rms * inv_rms * jnp.mean(gained * summed, axis=-1, keepdims=True)
    )
    grad_padded = padded_2(summed_grad.astype(jnp.bfloat16), (("lon", 1),), 1).astype(
        summed_grad.dtype
    )
    grad_latent = grid_grad[..., :channels] + grid_grad[..., channels:] + padded_mix(grad_padded)
    totals = lax.psum((grad_in, grad_out, grad_gain, head_grad), ("band", "lon"))
    return (
        grad_latent,
        totals[0] / devices_all,
        totals[1] / devices_all,
        totals[2] / devices_all,
        totals[3] / devices_all,
    )


def solution(mesh):
    return jax.shard_map(
        body,
        mesh=mesh,
        in_specs=(
            P("band", "lon", None),
            P("band", "lon", None),
            P(("band", "lon"), None, None),
            P(("band", "lon"), None),
            P(("band", "lon")),
            P(("band", "lon"), None, None),
            P(),
            P(),
            P(),
            P(),
        ),
        out_specs=(P("band", "lon", None), P(), P(), P(), P()),
        check_vma=False,
    )
```

profile of v0, /device:TPU:0, one launch (start us, length us, event | category | flops | bytes accessed | tf_op | source)
XLA Modules:
  0.0 370.8 jit_solution(1146212106312292507)
XLA Ops:
  7.2 0.0 copy-start
  7.2 2.8 copy.28
  10.0 0.5 collective-permute-start
  10.5 4.1 %collective-permute-start.1 = (bf16[32,1,256]{2,0,1:T(8,128)(2,1)S(1)}, bf16[32,1,256]{2,0,1:T(8,128)(2,1)S(1)}, u32[]{:S(2)}, u32[]{:S(2)}) collective-permute-start(bf16[32,1,256]{2,0,1:T(8,128)(2,1)S(1)} %get-tuple-element.25), channel_id=1, source_target_pairs={{1,0},{2,1},{3,2},{4,3},{5,4},{6,5},{7,6},{0,7},{9,8},{10,9},{11,1... | collective-permute-start | bytes 49160 | tf_op jit(solution)/shard_map/ppermute | solution.py:23
  14.7 1.3 collective-permute-done
  16.0 0.1 collective-permute-done.1
  16.1 0.3 maximum_convert_fusion
  16.4 0.0 copy-start.14
  16.4 0.8 multiply_reduce_fusion.2
  17.3 0.0 copy-start.3
  17.3 0.0 copy-start.18
  17.3 0.8 multiply_convert_fusion.3
  18.1 0.3 copy-done.18
  18.4 5.2 %multiply_convert_fusion.1 = (bf16[32,128,512]{2,1,0:T(8,128)(2,1)S(1)}, f32[32,128,512]{2,1,0:T(8,128)}) fusion(bf16[256,512]{1,0:T(8,128)(2,1)S(1)} %copy-done.18, bf16[32,128,256]{2,0,1:T(8,128)(2,1)S(1)} %multiply_convert_fusion.3), kind=kOutput, calls=%fused_computation.2 | convolution fusion | flops 1084227584 | bytes 14942208 | tf_op jit(solution)/shard_map/lmc,ch->lmh/dot_general | solution.py:99
  23.6 0.0 copy-done.9
  23.6 1.9 copy-done.6
  25.5 1.3 add_convert_fusion
  26.8 2.4 pad_maximum_fusion
  29.2 4.2 %gather_fusion = bf16[16,128,512]{2,1,0:T(8,128)(2,1)} fusion(bf16[32,128,512]{2,1,0:T(8,128)(2,1)} %pad_maximum_fusion, s32[1024]{0:T(1024)S(1)} %pad_clamp_fusion), kind=kCustom, calls=%fused_computation | custom fusion | bytes 4194368 | tf_op jit(solution)/shard_map/gather | solution.py:107
  33.4 4.8 %all-to-all-start = ((bf16[8,2,128,512]{3,2,1,0:T(8,128)(2,1)}), bf16[8,2,128,512]{3,2,1,0:T(8,128)(2,1)S(1)}, u32[]{:S(2)}, u32[]{:S(2)}) async-start(bf16[8,2,128,512]{3,2,1,0:T(8,128)(2,1)} %bitcast.70), calls=%async_computation | async-start | bytes 4194304 | tf_op jit(solution)/shard_map/all_to_all | solution.py:115
  38.2 0.0 copy-done.13
  38.2 0.0 copy-done.15
  38.2 0.1 fusion.37
  38.3 49.0 %all-to-all-done = bf16[8,2,128,512]{3,2,1,0:T(8,128)(2,1)S(1)} async-done(((bf16[8,2,128,512]{3,2,1,0:T(8,128)(2,1)}), bf16[8,2,128,512]{3,2,1,0:T(8,128)(2,1)S(1)}, u32[]{:S(2)}, u32[]{:S(2)}) %all-to-all-start) | async-done | bytes 2097184 | tf_op jit(solution)/shard_map/all_to_all | solution.py:115
  87.2 0.4 fusion.27
  87.7 0.8 add_convert_fusion.1
  88.5 0.0 copy-start.8
  88.5 0.0 copy-done.12
  88.5 0.5 fusion.11
  89.0 1.5 convolution_convert_fusion
  90.4 1.5 copy.32
  91.9 1.4 convolution_convert_fusion.2
  93.3 1.5 convolution_convert_fusion.1
  94.8 1.5 copy.34
  96.3 1.5 copy.35
  97.8 1.6 pad_maximum_fusion.1
  99.4 3.6 all-to-all-start.1
  103.0 0.2 all-reduce.3.cloned.1.call-start
  103.2 2.4 fusion.43
  105.6 46.4 %all-to-all-done.1 = bf16[8,2,128,512]{3,2,1,0:T(8,128)(2,1)S(1)} async-done(((bf16[8,2,128,512]{3,2,1,0:T(8,128)(2,1)}), bf16[8,2,128,512]{3,2,1,0:T(8,128)(2,1)S(1)}, u32[]{:S(2)}, u32[]{:S(2)}) %all-to-all-start.1) | async-done | bytes 2097184 | tf_op jit(solution)/shard_map/all_to_all | solution.py:128
  152.0 1.6 fusion.12
  153.6 0.3 slice.98
  153.9 4.9 %copy-done.7 = bf16[32,128,512]{2,1,0:T(8,128)(2,1)S(1)} copy-done((bf16[32,128,512]{2,1,0:T(8,128)(2,1)S(1)}, bf16[32,128,512]{2,1,0:T(8,128)(2,1)}, u32[]{:S(2)}) %copy-start.7) | copy-done | bytes 4194328
  158.8 3.6 fusion.23
  162.4 6.6 %multiply_convert_fusion = bf16[32,128,512]{2,1,0:T(8,128)(2,1)S(1)} fusion(f32[32,128,512]{2,1,0:T(8,128)} %get-tuple-element.27, bf16[32,128,256]{2,0,1:T(8,128)(2,1)S(1)} %slice.98, bf16[512,256]{1,0:T(8,128)(2,1)S(1)} %copy-done.11), kind=kOutput, calls=%fused_computation.1 | convolution fusion | flops 1092616192 | bytes 14942208 | tf_op jit(solution)/shard_map/lmc,hc->lmh/dot_general | solution.py:144
  168.9 1.9 copy-done.20
  170.9 3.7 fusion.20
  174.6 7.2 %multiply_reduce_fusion = (f32[256]{0:T(256)S(1)}, f32[32,128]{0,1:T(8,128)S(1)}, f32[32,128,256]{2,0,1:T(8,128)S(1)}) fusion(f32[32,128,256]{2,0,1:T(8,128)} %copy-done.3, f32[32,128]{0,1:T(8,128)S(1)} %add_rsqrt_fusion, f32[256]{0:T(256)S(1)} %copy-done.14, bf16[256,512]{1,0:T(8,128)(2,1)S(1)} %copy-done.19, bf16[32,128,512]{2,1,0:T(8,128)(2,1)} %copy-done.20), kind=kOutput, calls=%fused_computation.13 | convolution fusion | flops 1080028928 | bytes 12879872 | tf_op jit(solution)/shard_map/lmh,ch->lmc/dot_general | solution.py:147
  181.8 1.6 multiply_convert_fusion.2
  183.5 0.1 collective-permute-start.2
  183.5 3.5 collective-permute-start.3
  187.1 38.5 %psum.30 = f32[256]{0:T(256)S(1)} all-reduce(f32[256]{0:T(256)S(1)} %get-tuple-element.15), channel_id=1, replica_groups=mesh['band'=4,'lon'=8] {'band','lon'}, use_global_device_ids=true, to_apply=%region_5.6 | all-reduce | flops 256 | bytes 2048 | tf_op jit(solution)/shard_map/psum | solution.py:157
  225.5 0.6 broadcast_multiply_fusion.4
  226.1 0.0 all-reduce.3.cloned.1.call-update
  226.1 0.0 collective-permute-done.2
  226.1 0.0 collective-permute-done.3
  226.2 0.3 maximum_convert_fusion.1
  226.5 0.0 copy-start.1
  226.5 4.9 %fusion.2 = f32[32,128,256]{2,0,1:T(8,128)S(1)} fusion(f32[32,130,256]{2,0,1:T(8,128)S(1)} %maximum_convert_fusion.1, f32[32,128,512]{2,0,1:T(8,128)} %copy-done.2), kind=kLoop, calls=%fused_computation.7 | loop fusion | flops 5242880 | bytes 25165824 | tf_op jit(solution)/shard_map/add | solution.py:156
  231.4 4.4 %copy.43 = f32[32,128,256]{2,1,0:T(8,128)} copy(f32[32,128,256]{2,0,1:T(8,128)S(1)} %fusion.2) | data formatting | bytes 8388608
  235.8 122.8 %all-reduce.3.cloned.1.call-done = (f32[256,512]{1,0:T(8,128)}, f32[512,256]{1,0:T(8,128)}, f32[256,128]{1,0:T(8,128)}) async-done(((f32[256,512]{1,0:T(8,128)}, f32[512,256]{1,0:T(8,128)}, f32[256,128]{1,0:T(8,128)}), (f32[256,512]{1,0:T(8,128)}, f32[512,256]{1,0:T(8,128)}, f32[256,128]{1,0:T(8,128)})) %all-reduce.3.cloned.1.call-update) | async-done | bytes 1179664 | tf_op jit(solution)/shard_map/psum | solution.py:157
  358.7 1.9 broadcast_multiply_fusion
  360.5 1.9 broadcast_multiply_fusion.1
  362.4 1.6 broadcast_multiply_fusion.2
  (37 shorter events, 0.1 us)
Async XLA Ops:
  7.2 80.1 %copy-start = (bf16[16,128,128]{2,1,0:T(8,128)(2,1)S(1)}, bf16[16,128,128]{2,1,0:T(8,128)(2,1)}, u32[]{:S(2)}) copy-start(bf16[16,128,128]{2,1,0:T(8,128)(2,1)} %param.12) | copy-start | bytes 1572868
  7.2 7.5 %copy-start.16 = (s32[1,1,16]{2,1,0:T(1,128)S(1)}, s32[1,1,16]{2,1,0:T(1,128)}, u32[]{:S(2)}) copy-start(s32[1,1,16]{2,1,0:T(1,128)} %param.11) | copy-start | bytes 196
  10.0 6.0 %collective-permute-start = (bf16[32,1,256]{2,0,1:T(8,128)(2,1)S(1)}, bf16[32,1,256]{2,0,1:T(8,128)(2,1)S(1)}, u32[]{:S(2)}, u32[]{:S(2)}) collective-permute-start(bf16[32,1,256]{2,0,1:T(8,128)(2,1)S(1)} %get-tuple-element.24), channel_id=1, source_target_pairs={{0,1},{1,2},{2,3},{3,4},{4,5},{5,6},{6,7},{7,0},{8,9},{9,10},{10,1... | collective-permute-start | bytes 49160 | tf_op jit(solution)/shard_map/ppermute | solution.py:21
  10.5 5.5 %collective-permute-start.1 = (bf16[32,1,256]{2,0,1:T(8,128)(2,1)S(1)}, bf16[32,1,256]{2,0,1:T(8,128)(2,1)S(1)}, u32[]{:S(2)}, u32[]{:S(2)}) collective-permute-start(bf16[32,1,256]{2,0,1:T(8,128)(2,1)S(1)} %get-tuple-element.25), channel_id=1, source_target_pairs={{1,0},{2,1},{3,2},{4,3},{5,4},{6,5},{7,6},{0,7},{9,8},{10,9},{11,1... | collective-permute-start | bytes 49160 | tf_op jit(solution)/shard_map/ppermute | solution.py:23
  16.4 0.9 copy-start.14
  17.3 6.3 %copy-start.3 = (f32[32,128,256]{2,0,1:T(8,128)}, f32[32,128,256]{2,0,1:T(8,128)S(1)}, u32[]{:S(2)}) copy-start(f32[32,128,256]{2,0,1:T(8,128)S(1)} %get-tuple-element.21) | copy-start | bytes 12582916
  17.3 1.1 copy-start.18
  18.4 5.2 %copy-start.9 = (bf16[32,128,256]{2,0,1:T(8,128)(2,1)}, bf16[32,128,256]{2,0,1:T(8,128)(2,1)S(1)}, u32[]{:S(2)}) copy-start(bf16[32,128,256]{2,0,1:T(8,128)(2,1)S(1)} %multiply_convert_fusion.3) | copy-start | bytes 6291460
  18.4 7.1 %copy-start.5 = (bf16[32,128,256]{2,1,0:T(8,128)(2,1)S(1)}, bf16[32,128,256]{2,1,0:T(8,128)(2,1)}, u32[]{:S(2)}) copy-start(bf16[32,128,256]{2,1,0:T(8,128)(2,1)} %param.10) | copy-start | bytes 6291460
  18.4 7.1 %copy-start.11 = (bf16[512,256]{1,0:T(8,128)(2,1)S(1)}, bf16[512,256]{1,0:T(8,128)(2,1)}, u32[]{:S(2)}) copy-start(bf16[512,256]{1,0:T(8,128)(2,1)} %param.18) | copy-start | bytes 786436
  23.6 1.9 copy-start.6
  29.2 9.0 %copy-start.13 = (s32[16,128]{1,0:T(8,128)S(1)}, s32[16,128]{1,0:T(8,128)}, u32[]{:S(2)}) copy-start(s32[16,128]{1,0:T(8,128)} %param.13) | copy-start | bytes 24580
  29.2 9.0 %copy-start.15 = (s32[16]{0:T(128)S(1)}, s32[16]{0:T(128)}, u32[]{:S(2)}) copy-start(s32[16]{0:T(128)} %param.14) | copy-start | bytes 196
  33.4 53.9 %all-to-all-start = ((bf16[8,2,128,512]{3,2,1,0:T(8,128)(2,1)}), bf16[8,2,128,512]{3,2,1,0:T(8,128)(2,1)S(1)}, u32[]{:S(2)}, u32[]{:S(2)}) async-start(bf16[8,2,128,512]{3,2,1,0:T(8,128)(2,1)} %bitcast.70), calls=%async_computation | async-start | bytes 4194304 | tf_op jit(solution)/shard_map/all_to_all | solution.py:115
  87.2 1.2 copy-start.12
  87.2 1.2 copy-start.17
  88.5 2.0 copy-start.8
  99.4 52.6 %all-to-all-start.1 = ((bf16[8,2,128,512]{3,2,1,0:T(8,128)(2,1)}), bf16[8,2,128,512]{3,2,1,0:T(8,128)(2,1)S(1)}, u32[]{:S(2)}, u32[]{:S(2)}) async-start(bf16[8,2,128,512]{3,2,1,0:T(8,128)(2,1)} %pad_maximum_fusion.1), calls=%async_computation.1 | async-start | bytes 4194304 | tf_op jit(solution)/shard_map/all_to_all | solution.py:128
  103.0 255.7 %all-reduce.3.cloned.1.call-start = ((), (), s32[]{:S(2)}) async-start(), calls=%async_computation.2 | async-start | bytes 2359296 | tf_op jit(solution)/shard_map/psum | solution.py:157
  153.6 8.8 %copy-start.2 = (f32[32,128,512]{2,0,1:T(8,128)}, f32[32,128,512]{2,0,1:T(8,128)S(1)}, u32[]{:S(2)}) copy-start(f32[32,128,512]{2,0,1:T(8,128)S(1)} %fusion.12) | copy-start | bytes 25165828
  153.6 5.2 %copy-start.7 = (bf16[32,128,512]{2,1,0:T(8,128)(2,1)S(1)}, bf16[32,128,512]{2,1,0:T(8,128)(2,1)}, u32[]{:S(2)}) copy-start(bf16[32,128,512]{2,1,0:T(8,128)(2,1)} %copy-done.6) | copy-start | bytes 12582916
  162.4 8.5 %copy-start.10 = (bf16[32,128,256]{2,0,1:T(8,128)(2,1)S(1)}, bf16[32,128,256]{2,0,1:T(8,128)(2,1)}, u32[]{:S(2)}) copy-start(bf16[32,128,256]{2,0,1:T(8,128)(2,1)} %copy-done.9) | copy-start | bytes 6291460
  168.9 1.9 copy-start.20
  170.9 3.7 copy-start.19
  174.6 7.2 %copy-start.4 = (f32[32,128,256]{2,0,1:T(8,128)S(1)}, f32[32,128,256]{2,0,1:T(8,128)}, u32[]{:S(2)}) copy-start(f32[32,128,256]{2,0,1:T(8,128)} %copy-done.3) | copy-start | bytes 12582916
  183.5 42.7 %collective-permute-start.2 = (bf16[32,1,256]{2,0,1:T(8,128)(2,1)S(1)}, bf16[32,1,256]{2,0,1:T(8,128)(2,1)S(1)}, u32[]{:S(2)}, u32[]{:S(2)}) collective-permute-start(bf16[32,1,256]{2,0,1:T(8,128)(2,1)S(1)} %get-tuple-element.22), channel_id=1, source_target_pairs={{0,1},{1,2},{2,3},{3,4},{4,5},{5,6},{6,7},{7,0},{8,9},{9,10},{10,1... | collective-permute-start | bytes 49160 | tf_op jit(solution)/shard_map/ppermute | solution.py:21
  183.5 42.6 %collective-permute-start.3 = (bf16[32,1,256]{2,0,1:T(8,128)(2,1)S(1)}, bf16[32,1,256]{2,0,1:T(8,128)(2,1)S(1)}, u32[]{:S(2)}, u32[]{:S(2)}) collective-permute-start(bf16[32,1,256]{2,0,1:T(8,128)(2,1)S(1)} %get-tuple-element.23), channel_id=1, source_target_pairs={{1,0},{2,1},{3,2},{4,3},{5,4},{6,5},{7,6},{0,7},{9,8},{10,9},{11,1... | collective-permute-start | bytes 49160 | tf_op jit(solution)/shard_map/ppermute | solution.py:23
  226.5 137.5 %copy-start.1 = (bf16[16,128,128]{2,1,0:T(8,128)(2,1)S(1)}, bf16[16,128,128]{2,1,0:T(8,128)(2,1)}, u32[]{:S(2)}) copy-start(bf16[16,128,128]{2,1,0:T(8,128)(2,1)} %param.12) | copy-start | bytes 1572868
Sparse Core Ops, SparseCore 0:
  226.3 132.3 all-reduce.2
where the time goes:
time: 371 us
  waiting for transfers between devices  220 us (59%)
  blocking collectives  38.5 us (10%)
  matrix products  37.4 us (10%)
  local copies, waits for them, and re-layouts  25.4 us (7%)
  other arithmetic  18.7 us (5%)
  starting transfers between devices  16.8 us (5%)
  between operations  14.4 us (4%)
    psum x1, waiting for transfers between devices, body(): lax.psum((grad_in, grad_out, grad_gain, head_grad), ('band', 'lon'))  123 us
    all_to_all x1, waiting for transfers between devices, body(): lax.all_to_all(picked.reshape(peer_count, per_peer, lon_cells, 2 * channe...  49 us
    all_to_all x1, waiting for transfers between devices, body(): lax.all_to_all(tile_grads.reshape(peer_count, per_peer, lon_cells, 2 * ch...  46.4 us
    psum x1, blocking collectives, body(): lax.psum((grad_in, grad_out, grad_gain, head_grad), ('band', 'lon'))  38.5 us
    unnamed x44, local copies, waits for them, and re-layouts  16.4 us
    ppermute x2, starting transfers between devices, padded_2(): lax.ppermute(head, axis, [((i + 1) % count, i) for i in range(count)])  7.63 us
  transfers between devices with their start and end apart: 7, of which 5 were waited for; matrix products, arithmetic and copies ran while one was open for 3% of the time, Pallas kernels for 0%

commit v1 on v0

v1 whole, which is shorter than its diff:
```python
import functools
import math

import jax
import jax.numpy as jnp
from jax import lax
from jax.experimental import pallas as pl
from jax.experimental.pallas import tpu as pltpu
from jax.sharding import PartitionSpec as P

WINDOW_SLOTS = 7
norm_eps = 1e-05
f32, bf16 = jnp.float32, jnp.bfloat16
MESH = pl.DeviceIdType.MESH


def dot(a, b, dims=((1,), (0,))):
    return lax.dot_general(a, b, (dims, ((), ())), preferred_element_type=f32)


NN = ((1,), (0,))
NT = ((1,), (1,))
TN = ((0,), (0,))


def shifted(x, first, last):
    cells = x.shape[0]
    place = lax.broadcasted_iota(jnp.int32, x.shape, 0)
    before = jnp.where(place == 0, first, pltpu.roll(x, 1, 0))
    after = jnp.where(place == cells - 1, last, pltpu.roll(x, cells - 1, 0))
    return before + after


def layer_kernel(
    peers,
    lat_ref,
    rows_smem,
    rows_ref,
    w_ref,
    t_ref,
    slot_ref,
    count_ref,
    gain_ref,
    w_in_ref,
    w_out_ref,
    head_ref,
    part_ref,
    edge_ref,
    g_in,
    g_out,
    g_gain,
    g_head,
    wbuf,
    tbuf,
    aux,
    auxbuf,
    edge_f,
    edge_send,
    edge_recv,
    sel,
    u_s,
    inv_s,
    normed_s,
    act_s,
    slope_s,
    adv_s,
    sg_edge,
    send_w,
    send_t,
    send_a,
    recv_w,
    recv_t,
    recv_a,
    send_e,
    recv_e,
):
    lat_rows, cells, channels = lat_ref.shape
    blocks, obs = slot_ref.shape
    per = blocks // peers
    me = lax.axis_index("lon")
    right, left = lax.rem(me + 1, peers), lax.rem(me + peers - 1, peers)

    barrier = pltpu.get_barrier_semaphore()
    for d in range(1, peers):
        pl.semaphore_signal(
            barrier, inc=1, device_id={"lon": lax.rem(me + d, peers)}, device_id_type=MESH
        )
    pl.semaphore_wait(barrier, peers - 1)

    def exchange(d):
        to = lax.rem(me + d, peers)
        src, dst = pl.ds(to * per, per), pl.ds(me * per, per)
        copies = []
        for a, b, ss, rs in (
            (w_ref, wbuf, send_w, recv_w),
            (t_ref, tbuf, send_t, recv_t),
            (aux, auxbuf, send_a, recv_a),
        ):
            copies.append(
                pltpu.make_async_remote_copy(
                    src_ref=a.at[src],
                    dst_ref=b.at[dst],
                    send_sem=ss.at[to],
                    recv_sem=rs.at[me],
                    device_id={"lon": to},
                    device_id_type=MESH,
                )
            )
        return copies

    order = [peers // 2]
    for d in range(peers // 2 - 1, 0, -1):
        order += [d, peers - d]
    sends = {d: exchange(d) for d in order}
    for d in order:
        sends[d][0].start()
        sends[d][1].start()
    mine = pl.ds(me * per, per)
    pltpu.make_async_copy(w_ref.at[mine], wbuf.at[mine], recv_w.at[me]).start()
    pltpu.make_async_copy(t_ref.at[mine], tbuf.at[mine], recv_t.at[me]).start()

    coef = (slot_ref[...].astype(f32) / (WINDOW_SLOTS - 1)).astype(bf16).astype(f32)
    live = lax.broadcasted_iota(jnp.int32, (blocks, obs), 1) < count_ref[...]
    coded = jnp.where(live, coef, -1.0)
    aux[...] = jnp.broadcast_to(coded[:, None, :], aux.shape)
    for d in order:
        sends[d][2].start()
    pltpu.make_async_copy(aux.at[mine], auxbuf.at[mine], recv_a.at[me]).start()

    for r in range(lat_rows):
        edge_f[0, r : r + 1, :] = lat_ref[r, cells - 16 : cells, :].astype(f32)[15:16]
        edge_f[1, r : r + 1, :] = lat_ref[r, 0:16, :].astype(f32)[0:1]
    edge_send[0:2] = edge_f[...].astype(bf16)

    def edge_copy(phase, side):
        slot = 2 * phase + side
        return pltpu.make_async_remote_copy(
            src_ref=edge_send.at[slot],
            dst_ref=edge_recv.at[slot],
            send_sem=send_e.at[slot],
            recv_sem=recv_e.at[slot],
            device_id={"lon": left if side else right},
            device_id_type=MESH,
        )

    first_edges = [edge_copy(0, 0), edge_copy(0, 1)]
    for c in first_edges:
        c.start()

    g_in[...] = jnp.zeros_like(g_in)
    g_out[...] = jnp.zeros_like(g_out)
    g_gain[...] = jnp.zeros_like(g_gain)
    g_head[...] = jnp.zeros_like(g_head)
    gain = gain_ref[...]
    onehot = (
        rows_ref[...] == lax.broadcasted_iota(jnp.int32, (blocks, lat_rows), 1)
    ).astype(f32).astype(bf16)

    for c in first_edges:
        c.wait_recv()
    sel[0] = dot(onehot, edge_recv[0])
    sel[1] = dot(onehot, edge_recv[1])

    def forward(j, carry):
        tile = lat_ref[rows_smem[j]]
        x = tile.astype(f32)
        summed = x + 0.5 * shifted(x, sel[0, pl.ds(j, 1), :], sel[1, pl.ds(j, 1), :])
        inv = lax.rsqrt(jnp.mean(summed * summed, axis=-1, keepdims=True) + norm_eps)
        u = summed * inv
        normed = (u * gain).astype(bf16)
        pre = dot(normed, w_in_ref[...])
        sig = jax.nn.sigmoid(pre)
        act = (pre * sig).astype(bf16)
        u_s[j] = u
        inv_s[j] = inv
        normed_s[j] = normed
        act_s[j] = act
        slope_s[j] = sig * (1.0 + pre * (1.0 - sig))
        adv_s[j] = (x + dot(act, w_out_ref[...])).astype(bf16)
        return carry

    lax.fori_loop(0, blocks, forward, 0)

    eye = lax.broadcasted_iota(jnp.int32, (obs, obs), 0) == lax.broadcasted_iota(
        jnp.int32, (obs, obs), 1
    )
    loss_scale = 1.0 / math.sqrt(obs)

    def backward(i, carry):
        odd = lax.rem(i, 2)
        s = lax.rem(me + odd * ((i + 1) // 2) + (1 - odd) * (peers - i // 2), peers)
        base = s * per
        span = pl.ds(base, per)
        for buf, sem in ((wbuf, recv_w), (tbuf, recv_t), (auxbuf, recv_a)):
            pltpu.make_async_copy(buf.at[span], buf.at[span], sem.at[s]).wait()
        codes, lats = [], []
        for k in range(per):
            code = jnp.where(eye, auxbuf[base + k][0:1, :], 0.0)
            code = jnp.sum(code, axis=1, keepdims=True)
            codes.append(code)
            c = jnp.maximum(code, 0.0)
            w = wbuf[base + k]
            old = dot(w, lat_ref[rows_smem[base + k]])
            new = dot(w, adv_s[base + k])
            lats.append(((1.0 - c) * old + c * new).astype(bf16))
        obs_latent = jnp.concatenate(lats, axis=0)
        code = jnp.concatenate(codes, axis=0)
        c = jnp.maximum(code, 0.0)
        head = head_ref[...]
        predicted = dot(obs_latent, head)
        goals = tbuf[span].reshape(per * obs, head.shape[1]).astype(f32)
        residual = jnp.where(code >= 0.0, predicted - goals, 0.0)
        pred_grad = (residual * loss_scale).astype(bf16)
        g_head[...] += dot(obs_latent, pred_grad, TN)
        obs_grad = dot(pred_grad, head, NT).astype(bf16).astype(f32)
        back_old = ((1.0 - c) * obs_grad).astype(bf16)
        back_new = (c * obs_grad).astype(bf16)
        olds, news = [], []
        for k in range(per):
            w = wbuf[base + k]
            sl = slice(k * obs, (k + 1) * obs)
            olds.append(dot(w, back_old[sl], TN).astype(bf16))
            news.append(dot(w, back_new[sl], TN).astype(bf16))
        tile_new = jnp.concatenate(news, axis=0)
        act = act_s[span].reshape(per * cells, -1)
        slope = slope_s[span].reshape(per * cells, -1)
        normed = normed_s[span].reshape(per * cells, channels)
        u = u_s[span].reshape(per * cells, channels)
        g_out[...] += dot(act, tile_new, TN)
        pre_grad = (dot(tile_new, w_out_ref[...], NT) * slope).astype(bf16)
        g_in[...] += dot(normed, pre_grad, TN)
        normed_grad = dot(pre_grad, w_in_ref[...], NT)
        ng_u = normed_grad * u
        g_gain[...] += jnp.sum(ng_u, axis=0, keepdims=True)
        mean = jnp.mean(ng_u * gain, axis=-1, keepdims=True)
        core = normed_grad * gain - u * mean
        for k in range(per):
            sl = slice(k * cells, (k + 1) * cells)
            sg = inv_s[base + k] * core[sl]
            sg_edge[0, pl.ds(base + k, 1), :] = sg[cells - 1 : cells]
            sg_edge[1, pl.ds(base + k, 1), :] = sg[0:1]
            part_ref[base + k] = (
                olds[k].astype(f32) + news[k].astype(f32) + sg + 0.5 * shifted(sg, 0.0, 0.0)
            )
        return carry

    lax.fori_loop(0, peers, backward, 0)

    edge_send[2] = dot(onehot, sg_edge[0].astype(bf16), TN).astype(bf16)
    edge_send[3] = dot(onehot, sg_edge[1].astype(bf16), TN).astype(bf16)
    last_edges = [edge_copy(1, 0), edge_copy(1, 1)]
    for c in last_edges:
        c.start()
    for d in order:
        for c in sends[d]:
            c.wait_send()
    for c in first_edges:
        c.wait_send()
    for c in last_edges:
        c.wait()
    edge_ref[...] = 0.5 * edge_recv[2:4].astype(f32)


def layer(latent, rows, weights, slots, counts, targets, gain, w_in, w_out, head, peers):
    lat_rows, cells, channels = latent.shape
    blocks, obs = slots.shape
    hid = w_in.shape[1]
    values = head.shape[1]
    vmem, anym = pl.BlockSpec(memory_space=pltpu.VMEM), pl.BlockSpec(memory_space=pl.ANY)
    shape = jax.ShapeDtypeStruct
    dma = pltpu.SemaphoreType.DMA
    flops = 2 * blocks * cells * channels * (6 * hid + 4 * obs + 3 * values)
    return pl.pallas_call(
        functools.partial(layer_kernel, peers),
        out_shape=[
            shape((blocks, cells, channels), f32),
            shape((2, lat_rows, channels), f32),
            shape((channels, hid), f32),
            shape((hid, channels), f32),
            shape((1, channels), f32),
            shape((channels, values), f32),
        ],
        in_specs=[vmem, pl.BlockSpec(memory_space=pltpu.SMEM), vmem, anym, anym] + [vmem] * 6,
        out_specs=[vmem] * 6,
        scratch_shapes=[
            pltpu.VMEM((blocks, obs, cells), bf16),
            pltpu.VMEM((blocks, obs, values), bf16),
            pltpu.VMEM((blocks, 8, obs), f32),
            pltpu.VMEM((blocks, 8, obs), f32),
            pltpu.VMEM((2, lat_rows, channels), f32),
            pltpu.VMEM((4, lat_rows, channels), bf16),
            pltpu.VMEM((4, lat_rows, channels), bf16),
            pltpu.VMEM((2, blocks, channels), f32),
            pltpu.VMEM((blocks, cells, channels), f32),
            pltpu.VMEM((blocks, cells, 1), f32),
            pltpu.VMEM((blocks, cells, channels), bf16),
            pltpu.VMEM((blocks, cells, hid), bf16),
            pltpu.VMEM((blocks, cells, hid), f32),
            pltpu.VMEM((blocks, cells, channels), bf16),
            pltpu.VMEM((2, blocks, channels), f32),
        ]
        + [dma((peers,))] * 6
        + [dma((4,))] * 2,
        compiler_params=pltpu.CompilerParams(
            collective_id=0, has_side_effects=True, vmem_limit_bytes=48 * 1024 * 1024
        ),
        cost_estimate=pl.CostEstimate(
            flops=flops, bytes_accessed=10 * 1024 * 1024, transcendentals=blocks * cells * hid
        ),
    )(
        latent,
        rows,
        rows.reshape(blocks, 1),
        weights,
        targets,
        slots,
        counts.reshape(blocks, 1),
        gain.reshape(1, channels),
        w_in,
        w_out,
        head,
    )


def spread_kernel(step, rows_ref, part_ref, edge_ref, out_ref):
    blocks, cells, channels = part_ref.shape
    first = pl.program_id(0) * step
    out_ref[...] = jnp.zeros_like(out_ref)

    def add(j, carry):
        at = rows_ref[j] - first

        @pl.when((at >= 0) & (at < step))
        def _():
            out_ref[at] += part_ref[j]

        return carry

    lax.fori_loop(0, blocks, add, 0)
    for r in range(step):
        out_ref[r, 0:1, :] += edge_ref[0, pl.ds(first + r, 1), :]
        out_ref[r, cells - 1 : cells, :] += edge_ref[1, pl.ds(first + r, 1), :]


def spread(rows, part, edges, lat_rows):
    blocks, cells, channels = part.shape
    step = 4
    vmem = pl.BlockSpec(memory_space=pltpu.VMEM)
    return pl.pallas_call(
        functools.partial(spread_kernel, step),
        out_shape=jax.ShapeDtypeStruct((lat_rows, cells, channels), f32),
        grid=(lat_rows // step,),
        in_specs=[pl.BlockSpec(memory_space=pltpu.SMEM), vmem, vmem],
        out_specs=pl.BlockSpec((step, cells, channels), lambda i: (i, 0, 0)),
        compiler_params=pltpu.CompilerParams(vmem_limit_bytes=32 * 1024 * 1024),
        cost_estimate=pl.CostEstimate(
            flops=blocks * cells * channels,
            bytes_accessed=4 * (blocks + lat_rows) * cells * channels,
            transcendentals=0,
        ),
    )(rows, part, edges)


def body(latent, row_index, weights, slots, counts, targets, gain, w_in, w_out, head):
    peers = lax.axis_size("lon")
    devices_all = lax.axis_size("band") * peers
    rows = row_index.reshape(-1)
    part, edges, g_in, g_out, g_gain, g_head = layer(
        latent, rows, weights, slots, counts, targets, gain, w_in, w_out, head, peers
    )
    grad_latent = spread(rows, part, edges, latent.shape[0])
    totals = lax.psum((g_in, g_out, g_gain.reshape(-1), g_head), ("band", "lon"))
    return (grad_latent,) + tuple(total / devices_all for total in totals)


def solution(mesh):
    return jax.shard_map(
        body,
        mesh=mesh,
        in_specs=(
            P("band", "lon", None),
            P("band", "lon", None),
            P(("band", "lon"), None, None),
            P(("band", "lon"), None),
            P(("band", "lon")),
            P(("band", "lon"), None, None),
            P(),
            P(),
            P(),
            P(),
        ),
        out_specs=(P("band", "lon", None), P(), P(), P(), P()),
        check_vma=False,
    )
```

time: 371 us -> 214 us (0.58)
  waiting for transfers between devices: 220 us -> 86.1 us
  Pallas kernels: 0 us -> 56.1 us
  matrix products: 37.4 us -> 0 us
  local copies, waits for them, and re-layouts: 25.4 us -> 8.32 us
  starting transfers between devices: 16.8 us -> 0.04 us
  other arithmetic: 18.7 us -> 5.88 us
  blocking collectives: 38.5 us -> 42.6 us
    all_to_all x2 -> x0, waiting for transfers between devices: 95.3 us -> none  [the longest x1 49 us: body(): lax.all_to_all(picked.reshape(peer_count, per_peer, lon_cells, 2 * channe...]
    pallas_call x0 -> x2, Pallas kernels: none -> 56.1 us  [the longest x1 50.8 us: layer(): pl.pallas_call(functools.partial(layer_kernel, peers), out_shape=[shape((...]
    dot_general x14 -> x0, matrix products: 37.4 us -> none  [the longest x1 7.22 us: body(): jnp.einsum('lmh,ch->lmc', pre_grad, w_in, preferred_element_type=jnp.floa...]
    psum x1, waiting for transfers between devices: 123 us -> 86 us  [body(): lax.psum((g_in, g_out, g_gain.reshape(-1), g_head), ('band', 'lon'))]
    unnamed x44 -> x18, local copies, waits for them, and re-layouts: 16.4 us -> 6.85 us
    all_to_all x2 -> x0, starting transfers between devices: 8.4 us -> none  [the longest x1 4.79 us: body(): lax.all_to_all(picked.reshape(peer_count, per_peer, lon_cells, 2 * channe...]
    ppermute x4 -> x0, starting transfers between devices: 8.2 us -> none  [the longest x2 7.63 us: padded_2(): lax.ppermute(head, axis, [((i + 1) % count, i) for i in range(count)])]
    add x1 -> x0, other arithmetic: 4.87 us -> none  [body(): grid_grad[..., :channels] + grid_grad[..., channels:]]
  transfers between devices with their start and end apart: 7 -> 1, of which waited for: 5 -> 1; matrix products, arithmetic and copies ran while one was open for 3% -> 0% of each run, Pallas kernels for 0% -> 3%
where the time goes in v1:
time: 214 us; the launch traced here: 213 us
  waiting for transfers between devices  86.1 us (40%)
  Pallas kernels  56.1 us (26%)
  blocking collectives  42.6 us (20%)
  between operations  14.1 us (7%)
  local copies, waits for them, and re-layouts  8.32 us (4%)
  other arithmetic  5.88 us (3%)
    psum x1, waiting for transfers between devices, body(): lax.psum((g_in, g_out, g_gain.reshape(-1), g_head), ('band', 'lon'))  86 us
    pallas_call x1, Pallas kernels, layer(): pl.pallas_call(functools.partial(layer_kernel, peers), out_shape=[shape((...  50.8 us
    psum x1, blocking collectives, body(): lax.psum((g_in, g_out, g_gain.reshape(-1), g_head), ('band', 'lon'))  42.6 us
    unnamed x18, local copies, waits for them, and re-layouts  6.85 us
    div x4, other arithmetic, body(): return (grad_latent,) + tuple((total / devices_all for total in totals))  5.88 us
    pallas_call x1, Pallas kernels, spread(): pl.pallas_call(functools.partial(spread_kernel, step), out_shape=jax.Shap...  5.33 us
  transfers between devices with their start and end apart: 1, of which 1 were waited for; matrix products, arithmetic and copies ran while one was open for 0% of the time, Pallas kernels for 3%

profile of v1, /device:TPU:0, one launch (start us, length us, event | category | flops | bytes accessed | tf_op | source)
XLA Modules:
  0.0 213.0 jit_solution(13425764303870951862)
XLA Ops:
  7.2 0.0 all-reduce.3.cloned.1.call-start
  7.2 0.7 copy.16.count_ref
  7.9 0.7 copy.15.rows_ref
  8.7 0.0 copy-start
  8.7 0.7 copy-done
  9.3 0.0 copy-start.2
  9.3 1.0 copy-done.2
  10.4 0.0 copy-start.3
  10.4 1.0 copy-done.3
  11.4 0.0 copy-start.4
  11.4 0.9 copy-done.4
  12.4 0.0 copy-start.5
  12.4 0.9 copy-done.5
  13.3 0.0 copy-start.6
  13.3 0.8 copy-done.6
  14.2 0.0 copy-start.7
  14.2 0.7 copy-done.7
  14.9 0.0 copy-start.8
  14.9 0.7 copy-done.8
  15.5 0.0 copy-start.1
  15.5 50.8 %shard_map.137 = (f32[16,128,256]{2,1,0:T(8,128)S(1)}, f32[2,32,256]{2,1,0:T(8,128)S(1)}, f32[256,512]{1,0:T(8,128)}, f32[512,256]{1,0:T(8,128)}, f32[1,256]{1,0:T(1,128)S(1)}, /*index=5*/f32[256,128]{1,0:T(8,128)}) custom-call(bf16[32,128,256]{2,1,0:T(8,128)(2,1)} %lat_ref.1, s32[16]{0:T(128)S(1)} %bitcast.6, s32[16,1]{1,0:T(8,128)S(1)} %copy.15.rows_ref, ...), custom_call_target="tpu_custom_call" | custom-call | flops 4160749568 | bytes 10485760 | tf_op jit(solution)/shard_map/pallas_call | solution.py:273
  66.3 0.0 all-reduce.3.cloned.1.call-update
  66.3 0.0 copy-done.1
  66.3 5.3 %shard_map.138 = f32[32,128,256]{2,1,0:T(8,128)} custom-call(s32[16]{0:T(128)S(1)} %bitcast.7, f32[16,128,256]{2,1,0:T(8,128)S(1)} %get-tuple-element.11.part_ref, f32[2,32,256]{2,1,0:T(8,128)S(1)} %get-tuple-element.12.edge_ref), custom_call_target="tpu_custom_call" | custom-call | flops 524288 | bytes 6291456 | tf_op jit(solution)/shard_map/pallas_call | solution.py:349
  71.7 42.6 %psum.30 = f32[256]{0:T(256)S(1)} all-reduce(f32[256]{0:T(256)S(1)} %bitcast.8), channel_id=1, replica_groups=mesh['band'=4,'lon'=8] {'band','lon'}, use_global_device_ids=true, to_apply=%region_2.0 | all-reduce | flops 256 | bytes 2048 | tf_op jit(solution)/shard_map/psum | solution.py:372
  114.3 0.6 broadcast_multiply_fusion.3
  114.8 86.0 %all-reduce.3.cloned.1.call-done = (f32[256,512]{1,0:T(8,128)}, f32[512,256]{1,0:T(8,128)}, f32[256,128]{1,0:T(8,128)}) async-done(((f32[256,512]{1,0:T(8,128)}, f32[512,256]{1,0:T(8,128)}, f32[256,128]{1,0:T(8,128)}), (f32[256,512]{1,0:T(8,128)}, f32[512,256]{1,0:T(8,128)}, f32[256,128]{1,0:T(8,128)})) %all-reduce.3.cloned.1.call-update) | async-done | bytes 1179664 | tf_op jit(solution)/shard_map/psum | solution.py:372
  200.9 1.9 broadcast_multiply_fusion.1
  202.7 1.6 broadcast_multiply_fusion.2
  204.3 1.9 broadcast_multiply_fusion
Async XLA Ops:
  7.2 193.7 %all-reduce.3.cloned.1.call-start = ((), (), s32[]{:S(2)}) async-start(), calls=%async_computation | async-start | bytes 2359296 | tf_op jit(solution)/shard_map/psum | solution.py:372
  8.7 0.7 copy-start
  9.3 1.0 copy-start.2
  10.4 1.0 copy-start.3
  11.4 0.9 copy-start.4
  12.4 0.9 copy-start.5
  13.3 0.8 copy-start.6
  14.2 0.7 copy-start.7
  14.9 0.7 copy-start.8
  15.5 50.8 %copy-start.1 = (s32[1,1,16]{2,1,0:T(1,128)S(1)}, s32[1,1,16]{2,1,0:T(1,128)}, u32[]{:S(2)}) copy-start(s32[1,1,16]{2,1,0:T(1,128)} %param.11) | copy-start | bytes 196
Sparse Core Ops, SparseCore 0:
  66.5 134.3 all-reduce.2

commit v2 on v1

--- a/solution.py
+++ b/solution.py
@@ -33,23 +33,39 @@
 
 def layer_kernel(
     peers,
-    lat_ref,
+    bands,
     rows_smem,
-    rows_ref,
+    count_smem,
+    lat_hbm,
     w_ref,
     t_ref,
+    slot_hbm,
+    gain_hbm,
+    w_in_hbm,
+    w_out_hbm,
+    head_hbm,
+    part_ref,
+    edge_ref,
+    sums_ref,
+    lat_ref,
     slot_ref,
-    count_ref,
     gain_ref,
     w_in_ref,
     w_out_ref,
     head_ref,
-    part_ref,
-    edge_ref,
     g_in,
     g_out,
     g_gain,
     g_head,
+    onehot_f,
+    live_f,
+    acc,
+    from_core,
+    core_sum,
+    from_band,
+    band_sum,
+    from_lon,
+    total,
     wbuf,
     tbuf,
     aux,
@@ -73,19 +89,44 @@
     recv_a,
     send_e,
     recv_e,
+    load_sem,
+    core_sems,
+    band_sems,
+    lon_sems,
 ):
     lat_rows, cells, channels = lat_ref.shape
     blocks, obs = slot_ref.shape
     per = blocks // peers
     me = lax.axis_index("lon")
+    band = lax.axis_index("band")
     right, left = lax.rem(me + 1, peers), lax.rem(me + peers - 1, peers)
+
+    loads = [
+        pltpu.make_async_copy(a, b, load_sem.at[i])
+        for i, (a, b) in enumerate(
+            (
+                (slot_hbm, slot_ref),
+                (lat_hbm, lat_ref),
+                (gain_hbm, gain_ref),
+                (w_in_hbm, w_in_ref),
+                (w_out_hbm, w_out_ref),
+                (head_hbm, head_ref),
+            )
+        )
+    ]
+    for load in loads:
+        load.start()
 
     barrier = pltpu.get_barrier_semaphore()
     for d in range(1, peers):
         pl.semaphore_signal(
             barrier, inc=1, device_id={"lon": lax.rem(me + d, peers)}, device_id_type=MESH
         )
-    pl.semaphore_wait(barrier, peers - 1)
+    for d in range(1, bands):
+        pl.semaphore_signal(
+            barrier, inc=1, device_id={"band": lax.rem(band + d, bands)}, device_id_type=MESH
+        )
+    pl.semaphore_wait(barrier, peers + bands - 2)
 
     def exchange(d):
         to = lax.rem(me + d, peers)
@@ -119,14 +160,20 @@
     pltpu.make_async_copy(w_ref.at[mine], wbuf.at[mine], recv_w.at[me]).start()
     pltpu.make_async_copy(t_ref.at[mine], tbuf.at[mine], recv_t.at[me]).start()
 
+    lane = lax.broadcasted_iota(jnp.int32, (1, obs), 1)
+    row_lane = lax.broadcasted_iota(jnp.int32, (1, lat_rows), 1)
+    for j in range(blocks):
+        live_f[j : j + 1, :] = (lane < count_smem[j]).astype(f32)
+        onehot_f[j : j + 1, :] = (row_lane == rows_smem[0, 0, j]).astype(f32)
+    loads[0].wait()
     coef = (slot_ref[...].astype(f32) / (WINDOW_SLOTS - 1)).astype(bf16).astype(f32)
-    live = lax.broadcasted_iota(jnp.int32, (blocks, obs), 1) < count_ref[...]
-    coded = jnp.where(live, coef, -1.0)
+    coded = jnp.where(live_f[...] > 0.0, coef, -1.0)
     aux[...] = jnp.broadcast_to(coded[:, None, :], aux.shape)
     for d in order:
         sends[d][2].start()
     pltpu.make_async_copy(aux.at[mine], auxbuf.at[mine], recv_a.at[me]).start()
 
+    loads[1].wait()
     for r in range(lat_rows):
         edge_f[0, r : r + 1, :] = lat_ref[r, cells - 16 : cells, :].astype(f32)[15:16]
         edge_f[1, r : r + 1, :] = lat_ref[r, 0:16, :].astype(f32)[0:1]
@@ -151,35 +198,45 @@
     g_out[...] = jnp.zeros_like(g_out)
     g_gain[...] = jnp.zeros_like(g_gain)
     g_head[...] = jnp.zeros_like(g_head)
+    for load in loads[2:]:
+        load.wait()
     gain = gain_ref[...]
-    onehot = (
-        rows_ref[...] == lax.broadcasted_iota(jnp.int32, (blocks, lat_rows), 1)
-    ).astype(f32).astype(bf16)
+    onehot = onehot_f[...].astype(bf16)
 
     for c in first_edges:
         c.wait_recv()
     sel[0] = dot(onehot, edge_recv[0])
     sel[1] = dot(onehot, edge_recv[1])
 
-    def forward(j, carry):
-        tile = lat_ref[rows_smem[j]]
-        x = tile.astype(f32)
-        summed = x + 0.5 * shifted(x, sel[0, pl.ds(j, 1), :], sel[1, pl.ds(j, 1), :])
-        inv = lax.rsqrt(jnp.mean(summed * summed, axis=-1, keepdims=True) + norm_eps)
-        u = summed * inv
-        normed = (u * gain).astype(bf16)
-        pre = dot(normed, w_in_ref[...])
+    group = 2 * per if blocks % (2 * per) == 0 else per
+
+    def forward(i, carry):
+        xs, normeds = [], []
+        for k in range(group):
+            j = i * group + k
+            x = lat_ref[rows_smem[0, 0, j]].astype(f32)
+            summed = x + 0.5 * shifted(x, sel[0, pl.ds(j, 1), :], sel[1, pl.ds(j, 1), :])
+            inv = lax.rsqrt(jnp.mean(summed * summed, axis=-1, keepdims=True) + norm_eps)
+            u = summed * inv
+            normed = (u * gain).astype(bf16)
+            u_s[j] = u
+            inv_s[j] = inv
+            normed_s[j] = normed
+            xs.append(x)
+            normeds.append(normed)
+        pre = dot(jnp.concatenate(normeds, axis=0), w_in_ref[...])
         sig = jax.nn.sigmoid(pre)
         act = (pre * sig).astype(bf16)
-        u_s[j] = u
-        inv_s[j] = inv
-        normed_s[j] = normed
-        act_s[j] = act
-        slope_s[j] = sig * (1.0 + pre * (1.0 - sig))
-        adv_s[j] = (x + dot(act, w_out_ref[...])).astype(bf16)
+        slope = sig * (1.0 + pre * (1.0 - sig))
+        adv = (jnp.concatenate(xs, axis=0) + dot(act, w_out_ref[...])).astype(bf16)
+        for k in range(group):
+            j, sl = i * group + k, slice(k * cells, (k + 1) * cells)
+            act_s[j] = act[sl]
+            slope_s[j] = slope[sl]
+            adv_s[j] = adv[sl]
         return carry
 
-    lax.fori_loop(0, blocks, forward, 0)
+    lax.fori_loop(0, blocks // group, forward, 0)
 
     eye = lax.broadcasted_iota(jnp.int32, (obs, obs), 0) == lax.broadcasted_iota(
         jnp.int32, (obs, obs), 1
@@ -200,7 +257,7 @@
             codes.append(code)
             c = jnp.maximum(code, 0.0)
             w = wbuf[base + k]
-            old = dot(w, lat_ref[rows_smem[base + k]])
+            old = dot(w, lat_ref[rows_smem[0, 0, base + k]])
             new = dot(w, adv_s[base + k])
             lats.append(((1.0 - c) * old + c * new).astype(bf16))
         obs_latent = jnp.concatenate(lats, axis=0)
@@ -251,6 +308,85 @@
     last_edges = [edge_copy(1, 0), edge_copy(1, 1)]
     for c in last_edges:
         c.start()
+
+    hid, values = w_in_ref.shape[1], head_ref.shape[1]
+    at = 0
+    for grad in (g_in, g_out, g_head):
+        for first in range(0, grad.shape[1], 128):
+            acc[at : at + grad.shape[0], :] = grad[:, first : first + 128].astype(bf16)
+            at += grad.shape[0]
+    lines = [g_gain[:, i : i + 128] for i in range(0, channels, 128)]
+    lines.append(jnp.zeros((16 - len(lines), 128), f32))
+    acc[at : at + 16, :] = jnp.concatenate(lines, axis=0).astype(bf16)
+    if at + 16 < acc.shape[0]:
+        acc[at + 16 :, :] = jnp.zeros((acc.shape[0] - at - 16, 128), bf16)
+
+    core, rank, ranks = lax.rem(me, 2), me // 2, peers // 2
+    half = acc.shape[0] // 2
+    quarter = half // bands
+    piece = quarter // ranks
+
+    def rows_of(start, size):
+        return pl.ds(pl.multiple_of(start, 16), size)
+
+    def send(src, dst, sems, slot, to):
+        copy = pltpu.make_async_remote_copy(
+            src_ref=src,
+            dst_ref=dst,
+            send_sem=sems.at[0, slot],
+            recv_sem=sems.at[1, slot],
+            device_id=to,
+            device_id_type=MESH,
+        )
+        copy.start()
+        return copy
+
+    def finish(copies):
+        for copy in copies:
+            copy.wait()
+
+    sibling = {"lon": me + 1 - 2 * core}
+    finish([send(acc.at[rows_of((1 - core) * half, half)], from_core, core_sems, 0, sibling)])
+    core_sum[...] = (
+        acc[rows_of(core * half, half), :].astype(f32) + from_core[...].astype(f32)
+    ).astype(bf16)
+    copies = []
+    for d in range(1, bands):
+        to = lax.rem(band + d, bands)
+        src = core_sum.at[rows_of(to * quarter, quarter)]
+        copies.append(send(src, from_band.at[d - 1], band_sems, d - 1, {"band": to}))
+    finish(copies)
+    added = core_sum[rows_of(band * quarter, quarter), :].astype(f32)
+    for d in range(1, bands):
+        added = added + from_band[d - 1].astype(f32)
+    band_sum[...] = added.astype(bf16)
+    copies = []
+    for d in range(1, ranks):
+        to = lax.rem(rank + d, ranks)
+        src = band_sum.at[rows_of(to * piece, piece)]
+        copies.append(send(src, from_lon.at[d - 1], lon_sems, d - 1, {"lon": 2 * to + core}))
+    finish(copies)
+    added = band_sum[rows_of(rank * piece, piece), :].astype(f32)
+    for d in range(1, ranks):
+        added = added + from_lon[d - 1].astype(f32)
+    lot = core * half + band * quarter
+    own = rows_of(lot + rank * piece, piece)
+    total[own, :] = added.astype(bf16)
+    copies = []
+    for d in range(1, ranks):
+        to = {"lon": 2 * lax.rem(rank + d, ranks) + core}
+        copies.append(send(total.at[own], total.at[own], lon_sems, ranks + d - 2, to))
+    finish(copies)
+    own = rows_of(lot, quarter)
+    copies = []
+    for d in range(1, bands):
+        to = {"band": lax.rem(band + d, bands)}
+        copies.append(send(total.at[own], total.at[own], band_sems, bands + d - 2, to))
+    finish(copies)
+    own = rows_of(core * half, half)
+    finish([send(total.at[own], total.at[own], core_sems, 1, sibling)])
+    sums_ref[...] = total[...]
+
     for d in order:
         for c in sends[d]:
             c.wait_send()
@@ -261,28 +397,50 @@
     edge_ref[...] = 0.5 * edge_recv[2:4].astype(f32)
 
 
-def layer(latent, rows, weights, slots, counts, targets, gain, w_in, w_out, head, peers):
+def layer(latent, rows, weights, slots, counts, targets, gain, w_in, w_out, head, peers, bands):
     lat_rows, cells, channels = latent.shape
     blocks, obs = slots.shape
     hid = w_in.shape[1]
     values = head.shape[1]
     vmem, anym = pl.BlockSpec(memory_space=pltpu.VMEM), pl.BlockSpec(memory_space=pl.ANY)
+    smem = pl.BlockSpec(memory_space=pltpu.SMEM)
     shape = jax.ShapeDtypeStruct
     dma = pltpu.SemaphoreType.DMA
     flops = 2 * blocks * cells * channels * (6 * hid + 4 * obs + 3 * values)
+    packed = channels * (2 * hid + values) // 128 + 16
+    pieces = bands * peers
+    total = pieces * 16 * pl.cdiv(packed, pieces * 16)
+    half, quarter = total // 2, total // 2 // bands
+    piece, ranks = total // pieces, peers // 2
     return pl.pallas_call(
-        functools.partial(layer_kernel, peers),
+        functools.partial(layer_kernel, peers, bands),
         out_shape=[
             shape((blocks, cells, channels), f32),
             shape((2, lat_rows, channels), f32),
-            shape((channels, hid), f32),
-            shape((hid, channels), f32),
-            shape((1, channels), f32),
-            shape((channels, values), f32),
+            shape((total, 128), bf16),
         ],
-        in_specs=[vmem, pl.BlockSpec(memory_space=pltpu.SMEM), vmem, anym, anym] + [vmem] * 6,
-        out_specs=[vmem] * 6,
+        in_specs=[smem] * 2 + [anym] * 8,
+        out_specs=[vmem] * 3,
         scratch_shapes=[
+            pltpu.VMEM(latent.shape, bf16),
+            pltpu.VMEM((blocks, obs), jnp.int32),
+            pltpu.VMEM((1, channels), f32),
+            pltpu.VMEM(w_in.shape, bf16),
+            pltpu.VMEM(w_out.shape, bf16),
+            pltpu.VMEM(head.shape, bf16),
+            pltpu.VMEM(w_in.shape, f32),
+            pltpu.VMEM(w_out.shape, f32),
+            pltpu.VMEM((1, channels), f32),
+            pltpu.VMEM(head.shape, f32),
+            pltpu.VMEM((blocks, lat_rows), f32),
+            pltpu.VMEM((blocks, obs), f32),
+            pltpu.VMEM((total, 128), bf16),
+            pltpu.VMEM((half, 128), bf16),
+            pltpu.VMEM((half, 128), bf16),
+            pltpu.VMEM((bands - 1, quarter, 128), bf16),
+            pltpu.VMEM((quarter, 128), bf16),
+            pltpu.VMEM((ranks - 1, piece, 128), bf16),
+            pltpu.VMEM((total, 128), bf16),
             pltpu.VMEM((blocks, obs, cells), bf16),
             pltpu.VMEM((blocks, obs, values), bf16),
             pltpu.VMEM((blocks, 8, obs), f32),
@@ -300,21 +458,21 @@
             pltpu.VMEM((2, blocks, channels), f32),
         ]
         + [dma((peers,))] * 6
-        + [dma((4,))] * 2,
+        + [dma((4,))] * 2
+        + [dma((6,)), dma((2, 2)), dma((2, 2 * (bands - 1))), dma((2, 2 * (ranks - 1)))],
         compiler_params=pltpu.CompilerParams(
-            collective_id=0, has_side_effects=True, vmem_limit_bytes=48 * 1024 * 1024
+            collective_id=0, has_side_effects=True, vmem_limit_bytes=56 * 1024 * 1024
         ),
         cost_estimate=pl.CostEstimate(
             flops=flops, bytes_accessed=10 * 1024 * 1024, transcendentals=blocks * cells * hid
         ),
     )(
+        rows,
+        counts,
         latent,
-        rows,
-        rows.reshape(blocks, 1),
         weights,
         targets,
         slots,
-        counts.reshape(blocks, 1),
         gain.reshape(1, channels),
         w_in,
         w_out,
@@ -322,13 +480,15 @@
     )
 
 
-def spread_kernel(step, rows_ref, part_ref, edge_ref, out_ref):
+def spread_kernel(
+    step, scale, rows_ref, part_ref, edge_ref, sums_ref, out_ref, w_in_g, w_out_g, gain_g, head_g
+):
     blocks, cells, channels = part_ref.shape
     first = pl.program_id(0) * step
     out_ref[...] = jnp.zeros_like(out_ref)
 
     def add(j, carry):
-        at = rows_ref[j] - first
+        at = rows_ref[0, 0, j] - first
 
         @pl.when((at >= 0) & (at < step))
         def _():
@@ -341,36 +501,54 @@
         out_ref[r, 0:1, :] += edge_ref[0, pl.ds(first + r, 1), :]
         out_ref[r, cells - 1 : cells, :] += edge_ref[1, pl.ds(first + r, 1), :]
 
-
-def spread(rows, part, edges, lat_rows):
+    @pl.when(pl.program_id(0) == 0)
+    def _():
+        at = 0
+        for grad in (w_in_g, w_out_g, head_g):
+            for lane in range(0, grad.shape[1], 128):
+                part = sums_ref[at : at + grad.shape[0], :].astype(f32)
+                grad[:, lane : lane + 128] = part * scale
+                at += grad.shape[0]
+        lines = sums_ref[at : at + 16, :].astype(f32) * scale
+        for i in range(channels // 128):
+            gain_g[:, i * 128 : (i + 1) * 128] = lines[i : i + 1]
+
+
+def spread(rows, part, edges, sums, lat_rows, w_in, w_out, head, scale):
     blocks, cells, channels = part.shape
     step = 4
     vmem = pl.BlockSpec(memory_space=pltpu.VMEM)
+    shape = jax.ShapeDtypeStruct
     return pl.pallas_call(
-        functools.partial(spread_kernel, step),
-        out_shape=jax.ShapeDtypeStruct((lat_rows, cells, channels), f32),
+        functools.partial(spread_kernel, step, scale),
+        out_shape=[
+            shape((lat_rows, cells, channels), f32),
+            shape(w_in.shape, f32),
+            shape(w_out.shape, f32),
+            shape((1, channels), f32),
+            shape(head.shape, f32),
+        ],
         grid=(lat_rows // step,),
-        in_specs=[pl.BlockSpec(memory_space=pltpu.SMEM), vmem, vmem],
-        out_specs=pl.BlockSpec((step, cells, channels), lambda i: (i, 0, 0)),
+        in_specs=[pl.BlockSpec(memory_space=pltpu.SMEM), vmem, vmem, vmem],
+        out_specs=[pl.BlockSpec((step, cells, channels), lambda i: (i, 0, 0))] + [vmem] * 4,
         compiler_params=pltpu.CompilerParams(vmem_limit_bytes=32 * 1024 * 1024),
         cost_estimate=pl.CostEstimate(
             flops=blocks * cells * channels,
             bytes_accessed=4 * (blocks + lat_rows) * cells * channels,
             transcendentals=0,
         ),
-    )(rows, part, edges)
+    )(rows, part, edges, sums)
 
 
 def body(latent, row_index, weights, slots, counts, targets, gain, w_in, w_out, head):
-    peers = lax.axis_size("lon")
-    devices_all = lax.axis_size("band") * peers
-    rows = row_index.reshape(-1)
-    part, edges, g_in, g_out, g_gain, g_head = layer(
-        latent, rows, weights, slots, counts, targets, gain, w_in, w_out, head, peers
+    peers, bands = lax.axis_size("lon"), lax.axis_size("band")
+    part, edges, sums = layer(
+        latent, row_index, weights, slots, counts, targets, gain, w_in, w_out, head, peers, bands
     )
-    grad_latent = spread(rows, part, edges, latent.shape[0])
-    totals = lax.psum((g_in, g_out, g_gain.reshape(-1), g_head), ("band", "lon"))
-    return (grad_latent,) + tuple(total / devices_all for total in totals)
+    grad_latent, g_in, g_out, g_gain, g_head = spread(
+        row_index, part, edges, sums, latent.shape[0], w_in, w_out, head, 1.0 / (peers * bands)
+    )
+    return grad_latent, g_in, g_out, g_gain.reshape(-1), g_head
 
 
 def solution(mesh):

time: 214 us -> 79.4 us (0.37)
  waiting for transfers between devices: 86.1 us -> 0 us
  blocking collectives: 42.6 us -> 0 us
  Pallas kernels: 56.1 us -> 75 us
  between operations: 14.1 us -> 0.67 us
  other arithmetic: 5.88 us -> 0 us
  local copies, waits for them, and re-layouts: 8.32 us -> 3.51 us
    psum x1 -> x0, waiting for transfers between devices: 86 us -> none  [body(): lax.psum((g_in, g_out, g_gain.reshape(-1), g_head), ('band', 'lon'))]
    psum x1 -> x0, blocking collectives: 42.6 us -> none  [body(): lax.psum((g_in, g_out, g_gain.reshape(-1), g_head), ('band', 'lon'))]
    pallas_call x2, Pallas kernels: 56.1 us -> 75 us  [the longest x1 69.2 us: layer(): pl.pallas_call(functools.partial(layer_kernel, peers, bands), out_shape=[...]
    div x4 -> x0, other arithmetic: 5.88 us -> none  [body(): return (grad_latent,) + tuple((total / devices_all for total in totals))]
    unnamed x18 -> x8, local copies, waits for them, and re-layouts: 6.85 us -> 3.51 us
  transfers between devices with their start and end apart: 1 -> 0, of which waited for: 1 -> 0; matrix products, arithmetic and copies ran while one was open for 0% -> 0% of each run, Pallas kernels for 3% -> 0%
where the time goes in v2:
time: 79.4 us; the launch traced here: 79.2 us
  Pallas kernels  75 us (94%)
  local copies, waits for them, and re-layouts  3.51 us (4%)
    pallas_call x1, Pallas kernels, layer(): pl.pallas_call(functools.partial(layer_kernel, peers, bands), out_shape=[...  69.2 us
    pallas_call x1, Pallas kernels, spread(): pl.pallas_call(functools.partial(spread_kernel, step, scale), out_shape=[...  5.83 us
    unnamed x8, local copies, waits for them, and re-layouts  3.51 us

profile of v2, /device:TPU:0, one launch (start us, length us, event | category | flops | bytes accessed | tf_op | source)
XLA Modules:
  0.0 79.2 jit_solution(907540078307433434)
XLA Ops:
  0.6 0.0 copy-start.3
  0.6 69.2 %shard_map.137 = (f32[16,128,256]{2,1,0:T(8,128)}, f32[2,32,256]{2,1,0:T(8,128)}, bf16[2560,128]{1,0:T(8,128)(2,1)}) custom-call(s32[1,1,16]{2,1,0:T(1,128)} %rows_ref.1, s32[16]{0:T(128)} %count_smem.1, bf16[32,128,256]{2,1,0:T(8,128)(2,1)} %lat_hbm.1, bf16[16,128,128]{2,1,0:T(8,128)(2,1)} %w_ref.1, bf16[16,128,128]{2,1,0:T(8,128)(2,1)} %t_ref.1, ...), custom_call_target="tpu_custom_call" | custom-call | flops 4160749568 | bytes 10485760 | tf_op jit(solution)/shard_map/pallas_call | solution.py:415
  69.8 0.0 copy-done.3
  69.8 0.0 copy-start
  69.8 1.6 %copy-done = f32[16,128,256]{2,1,0:T(8,128)S(1)} copy-done((f32[16,128,256]{2,1,0:T(8,128)S(1)}, f32[16,128,256]{2,1,0:T(8,128)}, u32[]{:S(2)}) %copy-start) | copy-done | bytes 2097176
  71.4 0.0 copy-start.1
  71.4 1.1 %copy-done.1 = bf16[2560,128]{1,0:T(8,128)(2,1)S(1)} copy-done((bf16[2560,128]{1,0:T(8,128)(2,1)S(1)}, bf16[2560,128]{1,0:T(8,128)(2,1)}, u32[]{:S(2)}) %copy-start.1) | copy-done | bytes 655384
  72.5 0.0 copy-start.2
  72.5 0.8 %copy-done.2 = f32[2,32,256]{2,1,0:T(8,128)S(1)} copy-done((f32[2,32,256]{2,1,0:T(8,128)S(1)}, f32[2,32,256]{2,1,0:T(8,128)}, u32[]{:S(2)}) %copy-start.2) | copy-done | bytes 65560
  73.3 5.8 %shard_map.138 = (f32[32,128,256]{2,1,0:T(8,128)}, f32[256,512]{1,0:T(8,128)}, f32[512,256]{1,0:T(8,128)}, f32[1,256]{1,0:T(1,128)}, f32[256,128]{1,0:T(8,128)}) custom-call(s32[1,1,16]{2,1,0:T(1,128)S(1)} %copy-done.3, f32[16,128,256]{2,1,0:T(8,128)S(1)} %copy-done, f32[2,32,256]{2,1,0:T(8,128)S(1)} %copy-done.2, bf16[2560,128]{1,0:T(8,128)(2,1)S(1)} %copy-done.1), custom_call_target="tpu_custom_call" | custom-call | flops 524288 | bytes 6291456 | tf_op jit(solution)/shard_map/pallas_call | solution.py:522
Async XLA Ops:
  0.6 69.2 %copy-start.3 = (s32[1,1,16]{2,1,0:T(1,128)S(1)}, s32[1,1,16]{2,1,0:T(1,128)}, u32[]{:S(2)}) copy-start(s32[1,1,16]{2,1,0:T(1,128)} %rows_ref.1) | copy-start | bytes 196
  69.8 1.6 %copy-start = (f32[16,128,256]{2,1,0:T(8,128)S(1)}, f32[16,128,256]{2,1,0:T(8,128)}, u32[]{:S(2)}) copy-start(f32[16,128,256]{2,1,0:T(8,128)} %get-tuple-element.13.part_ref) | copy-start | bytes 6291460
  71.4 1.1 %copy-start.1 = (bf16[2560,128]{1,0:T(8,128)(2,1)S(1)}, bf16[2560,128]{1,0:T(8,128)(2,1)}, u32[]{:S(2)}) copy-start(bf16[2560,128]{1,0:T(8,128)(2,1)} %get-tuple-element.15.sums_ref) | copy-start | bytes 1966084
  72.5 0.8 %copy-start.2 = (f32[2,32,256]{2,1,0:T(8,128)S(1)}, f32[2,32,256]{2,1,0:T(8,128)}, u32[]{:S(2)}) copy-start(f32[2,32,256]{2,1,0:T(8,128)} %get-tuple-element.14.edge_ref) | copy-start | bytes 196612

commit v3 on v2

v3 whole, which is shorter than its diff:
```python
import functools
import math

import jax
import jax.numpy as jnp
from jax import lax
from jax.experimental import pallas as pl
from jax.experimental.pallas import tpu as pltpu
from jax.sharding import PartitionSpec as P

WINDOW_SLOTS = 7
norm_eps = 1e-05
f32, bf16 = jnp.float32, jnp.bfloat16
MESH = pl.DeviceIdType.MESH


def dot(a, b, dims=((1,), (0,))):
    return lax.dot_general(a, b, (dims, ((), ())), preferred_element_type=f32)


NN = ((1,), (0,))
NT = ((1,), (1,))
TN = ((0,), (0,))


def shifted(x, first, last):
    cells = x.shape[0]
    place = lax.broadcasted_iota(jnp.int32, x.shape, 0)
    before = jnp.where(place == 0, first, pltpu.roll(x, 1, 0))
    after = jnp.where(place == cells - 1, last, pltpu.roll(x, cells - 1, 0))
    return before + after


def layer_kernel(
    peers,
    bands,
    rows_smem,
    count_smem,
    lat_hbm,
    w_ref,
    t_ref,
    slot_hbm,
    gain_hbm,
    w_in_hbm,
    w_out_hbm,
    head_hbm,
    rows_out,
    sums_ref,
    part_ref,
    lat_out,
    lat_ref,
    slot_ref,
    gain_ref,
    w_in_ref,
    w_out_ref,
    head_ref,
    g_in,
    g_out,
    g_gain,
    g_head,
    onehot_f,
    live_f,
    chunk_a,
    chunk_b,
    wbuf,
    tbuf,
    aux,
    auxbuf,
    edge_f,
    edge_send,
    edge_recv,
    sel,
    u_s,
    inv_s,
    normed_s,
    act_s,
    slope_s,
    adv_s,
    sg_edge,
    send_w,
    send_t,
    send_a,
    recv_w,
    recv_t,
    recv_a,
    send_e,
    recv_e,
    load_sem,
    store_sem,
    core_sems,
    band_sems,
    lon_sems,
):
    lat_rows, cells, channels = lat_ref.shape
    blocks, obs = slot_ref.shape
    per = blocks // peers
    me = lax.axis_index("lon")
    band = lax.axis_index("band")
    right, left = lax.rem(me + 1, peers), lax.rem(me + peers - 1, peers)

    def partner(m):
        other, bit = me, 1
        while bit < peers:
            flip = (m // bit) % 2
            other = other + flip * bit * (1 - 2 * ((me // bit) % 2))
            bit *= 2
        return other

    loads = [
        pltpu.make_async_copy(a, b, load_sem.at[i])
        for i, (a, b) in enumerate(
            (
                (slot_hbm, slot_ref),
                (lat_hbm, lat_ref),
                (gain_hbm, gain_ref),
                (w_in_hbm, w_in_ref),
                (w_out_hbm, w_out_ref),
                (head_hbm, head_ref),
            )
        )
    ]
    for load in loads:
        load.start()

    lane = lax.broadcasted_iota(jnp.int32, (1, obs), 1)
    row_lane = lax.broadcasted_iota(jnp.int32, (1, lat_rows), 1)
    for j in range(blocks):
        live_f[j : j + 1, :] = (lane < count_smem[j]).astype(f32)
        onehot_f[j : j + 1, :] = (row_lane == rows_smem[0, 0, j]).astype(f32)
    loads[0].wait()
    coef = (slot_ref[...].astype(f32) / (WINDOW_SLOTS - 1)).astype(bf16).astype(f32)
    coded = jnp.where(live_f[...] > 0.0, coef, -1.0)
    aux[...] = jnp.broadcast_to(coded[:, None, :], aux.shape)
    loads[1].wait()
    for r in range(lat_rows):
        edge_f[0, r : r + 1, :] = lat_ref[r, cells - 16 : cells, :].astype(f32)[15:16]
        edge_f[1, r : r + 1, :] = lat_ref[r, 0:16, :].astype(f32)[0:1]
    edge_send[0:2] = edge_f[...].astype(bf16)

    barrier = pltpu.get_barrier_semaphore()
    for d in range(1, peers):
        pl.semaphore_signal(
            barrier, inc=1, device_id={"lon": lax.rem(me + d, peers)}, device_id_type=MESH
        )
    for d in range(1, bands):
        pl.semaphore_signal(
            barrier, inc=1, device_id={"band": lax.rem(band + d, bands)}, device_id_type=MESH
        )
    pl.semaphore_wait(barrier, peers + bands - 2)

    def edge_copy(phase, side):
        slot = 2 * phase + side
        return pltpu.make_async_remote_copy(
            src_ref=edge_send.at[slot],
            dst_ref=edge_recv.at[slot],
            send_sem=send_e.at[slot],
            recv_sem=recv_e.at[slot],
            device_id={"lon": left if side else right},
            device_id_type=MESH,
        )

    first_edges = [edge_copy(0, 0), edge_copy(0, 1)]
    for c in first_edges:
        c.start()

    def exchange(m):
        to = partner(m)
        src, dst = pl.ds(to * per, per), pl.ds(me * per, per)
        return [
            pltpu.make_async_remote_copy(
                src_ref=a.at[src],
                dst_ref=b.at[dst],
                send_sem=ss.at[to],
                recv_sem=rs.at[me],
                device_id={"lon": to},
                device_id_type=MESH,
            )
            for a, b, ss, rs in (
                (aux, auxbuf, send_a, recv_a),
                (w_ref, wbuf, send_w, recv_w),
                (t_ref, tbuf, send_t, recv_t),
            )
        ]

    sends = [None] + [exchange(m) for m in range(1, peers)]
    for m in range(1, peers):
        sends[m][0].start()
    mine = pl.ds(me * per, per)
    pltpu.make_async_copy(aux.at[mine], auxbuf.at[mine], recv_a.at[me]).start()
    pltpu.make_async_copy(w_ref.at[mine], wbuf.at[mine], recv_w.at[me]).start()
    pltpu.make_async_copy(t_ref.at[mine], tbuf.at[mine], recv_t.at[me]).start()
    far = list(range(peers // 2, peers - 1))
    order = [1]
    for m in range(2, peers // 2):
        order += [far.pop(0), m]
    for m in order + far:
        sends[m][1].start()
        sends[m][2].start()

    g_in[...] = jnp.zeros_like(g_in)
    g_out[...] = jnp.zeros_like(g_out)
    g_gain[...] = jnp.zeros_like(g_gain)
    g_head[...] = jnp.zeros_like(g_head)
    for load in loads[2:]:
        load.wait()
    gain = gain_ref[...]
    onehot = onehot_f[...].astype(bf16)

    for c in first_edges:
        c.wait_recv()
    sel[0] = dot(onehot, edge_recv[0])
    sel[1] = dot(onehot, edge_recv[1])

    group = 2 * per if blocks % (2 * per) == 0 else per

    def forward(i, carry):
        xs, normeds = [], []
        for k in range(group):
            j = i * group + k
            x = lat_ref[rows_smem[0, 0, j]].astype(f32)
            summed = x + 0.5 * shifted(x, sel[0, pl.ds(j, 1), :], sel[1, pl.ds(j, 1), :])
            inv = lax.rsqrt(jnp.mean(summed * summed, axis=-1, keepdims=True) + norm_eps)
            u = summed * inv
            normed = (u * gain).astype(bf16)
            u_s[j] = u
            inv_s[j] = inv
            normed_s[j] = normed
            xs.append(x)
            normeds.append(normed)
        pre = dot(jnp.concatenate(normeds, axis=0), w_in_ref[...])
        sig = jax.nn.sigmoid(pre)
        act = (pre * sig).astype(bf16)
        slope = sig * (1.0 + pre * (1.0 - sig))
        adv = (jnp.concatenate(xs, axis=0) + dot(act, w_out_ref[...])).astype(bf16)
        for k in range(group):
            j, sl = i * group + k, slice(k * cells, (k + 1) * cells)
            act_s[j] = act[sl]
            slope_s[j] = slope[sl]
            adv_s[j] = adv[sl]
        return carry

    lax.fori_loop(0, blocks // group, forward, 0)

    eye = lax.broadcasted_iota(jnp.int32, (obs, obs), 0) == lax.broadcasted_iota(
        jnp.int32, (obs, obs), 1
    )
    loss_scale = 1.0 / math.sqrt(obs)

    def backward(i, carry):
        s, bit = me, 1
        while bit < peers:
            s = s + lax.rem(i // bit, 2) * bit * (1 - 2 * ((me // bit) % 2))
            bit *= 2

        @pl.when(i == peers // 2 - 2)
        def _():
            sends[peers - 1][1].start()
            sends[peers - 1][2].start()

        base = s * per
        span = pl.ds(base, per)
        for buf, sem in ((wbuf, recv_w), (tbuf, recv_t), (auxbuf, recv_a)):
            pltpu.make_async_copy(buf.at[span], buf.at[span], sem.at[s]).wait()
        codes, lats = [], []
        for k in range(per):
            code = jnp.where(eye, auxbuf[base + k][0:1, :], 0.0)
            code = jnp.sum(code, axis=1, keepdims=True)
            codes.append(code)
            c = jnp.maximum(code, 0.0)
            w = wbuf[base + k]
            old = dot(w, lat_ref[rows_smem[0, 0, base + k]])
            new = dot(w, adv_s[base + k])
            lats.append(((1.0 - c) * old + c * new).astype(bf16))
        obs_latent = jnp.concatenate(lats, axis=0)
        code = jnp.concatenate(codes, axis=0)
        c = jnp.maximum(code, 0.0)
        head = head_ref[...]
        predicted = dot(obs_latent, head)
        goals = tbuf[span].reshape(per * obs, head.shape[1]).astype(f32)
        residual = jnp.where(code >= 0.0, predicted - goals, 0.0)
        pred_grad = (residual * loss_scale).astype(bf16)
        g_head[...] += dot(obs_latent, pred_grad, TN)
        obs_grad = dot(pred_grad, head, NT).astype(bf16).astype(f32)
        back_old = ((1.0 - c) * obs_grad).astype(bf16)
        back_new = (c * obs_grad).astype(bf16)
        olds, news = [], []
        for k in range(per):
            w = wbuf[base + k]
            sl = slice(k * obs, (k + 1) * obs)
            olds.append(dot(w, back_old[sl], TN).astype(bf16))
            news.append(dot(w, back_new[sl], TN).astype(bf16))
        tile_new = jnp.concatenate(news, axis=0)
        act = act_s[span].reshape(per * cells, -1)
        slope = slope_s[span].reshape(per * cells, -1)
        normed = normed_s[span].reshape(per * cells, channels)
        u = u_s[span].reshape(per * cells, channels)
        g_out[...] += dot(act, tile_new, TN)
        pre_grad = (dot(tile_new, w_out_ref[...], NT) * slope).astype(bf16)
        g_in[...] += dot(normed, pre_grad, TN)
        normed_grad = dot(pre_grad, w_in_ref[...], NT)
        ng_u = normed_grad * u
        g_gain[...] += jnp.sum(ng_u, axis=0, keepdims=True)
        mean = jnp.mean(ng_u * gain, axis=-1, keepdims=True)
        core = normed_grad * gain - u * mean
        for k in range(per):
            sl = slice(k * cells, (k + 1) * cells)
            sg = inv_s[base + k] * core[sl]
            sg_edge[0, pl.ds(base + k, 1), :] = sg[cells - 1 : cells]
            sg_edge[1, pl.ds(base + k, 1), :] = sg[0:1]
            part_ref[base + k] = (
                olds[k].astype(f32) + news[k].astype(f32) + sg + 0.5 * shifted(sg, 0.0, 0.0)
            )
        return carry

    lax.fori_loop(0, peers, backward, 0)

    edge_send[2] = dot(onehot, sg_edge[0].astype(bf16), TN).astype(bf16)
    edge_send[3] = dot(onehot, sg_edge[1].astype(bf16), TN).astype(bf16)
    last_edges = [edge_copy(1, 0), edge_copy(1, 1)]
    for c in last_edges:
        c.start()


    def pack(acc, grads, tail):
        at = 0
        for grad in grads:
            for first in range(0, grad.shape[1], 128):
                acc[at : at + grad.shape[0], :] = grad[:, first : first + 128].astype(bf16)
                at += grad.shape[0]
        if tail:
            lines = [g_gain[:, i : i + 128] for i in range(0, channels, 128)]
            lines.append(jnp.zeros((16 - len(lines), 128), f32))
            acc[at : at + 16, :] = jnp.concatenate(lines, axis=0).astype(bf16)
            at += 16
        if at < acc.shape[0]:
            acc[at:, :] = jnp.zeros((acc.shape[0] - at, 128), bf16)

    core, rank, ranks = lax.rem(me, 2), me // 2, peers // 2
    sibling = {"lon": me + 1 - 2 * core}
    band_to = [{"band": lax.rem(band + d, bands)} for d in range(1, bands)]
    rank_to = [{"lon": 2 * lax.rem(rank + d, ranks) + core} for d in range(1, ranks)]
    started = []

    def rows_of(start, size):
        return pl.ds(pl.multiple_of(start, 16), size)

    def send(src, dst, sems, chunk, slot, to):
        copy = pltpu.make_async_remote_copy(
            src_ref=src,
            dst_ref=dst,
            send_sem=sems.at[chunk, 0, slot],
            recv_sem=sems.at[chunk, 1, slot],
            device_id=to,
            device_id_type=MESH,
        )
        copy.start()
        started.append(copy)
        return copy

    def arrived(copies):
        for copy in copies:
            copy.wait_recv()

    def reduce_steps(n, chunk):
        acc, from_core, core_sum, from_band, band_sum, from_lon, total = chunk
        half = acc.shape[0] // 2
        quarter = half // bands
        piece = quarter // ranks
        lot = core * half + band * quarter
        got = [send(acc.at[rows_of((1 - core) * half, half)], from_core, core_sems, n, 0, sibling)]
        yield
        arrived(got)
        core_sum[...] = (
            acc[rows_of(core * half, half), :].astype(f32) + from_core[...].astype(f32)
        ).astype(bf16)
        got = []
        for d in range(1, bands):
            src = core_sum.at[rows_of(lax.rem(band + d, bands) * quarter, quarter)]
            got.append(send(src, from_band.at[d - 1], band_sems, n, d - 1, band_to[d - 1]))
        yield
        arrived(got)
        added = core_sum[rows_of(band * quarter, quarter), :].astype(f32)
        for d in range(1, bands):
            added = added + from_band[d - 1].astype(f32)
        band_sum[...] = added.astype(bf16)
        got = []
        for d in range(1, ranks):
            src = band_sum.at[rows_of(lax.rem(rank + d, ranks) * piece, piece)]
            got.append(send(src, from_lon.at[d - 1], lon_sems, n, d - 1, rank_to[d - 1]))
        yield
        arrived(got)
        added = band_sum[rows_of(rank * piece, piece), :].astype(f32)
        for d in range(1, ranks):
            added = added + from_lon[d - 1].astype(f32)
        own = rows_of(lot + rank * piece, piece)
        total[own, :] = added.astype(bf16)
        own = total.at[own]
        got = []
        for d in range(1, ranks):
            got.append(send(own, own, lon_sems, n, ranks + d - 2, rank_to[d - 1]))
        yield
        arrived(got)
        own = total.at[rows_of(lot, quarter)]
        got = []
        for d in range(1, bands):
            got.append(send(own, own, band_sems, n, bands + d - 2, band_to[d - 1]))
        yield
        arrived(got)
        own = total.at[rows_of(core * half, half)]
        got = [send(own, own, core_sems, n, 1, sibling)]
        yield
        arrived(got)
        yield

    pack(chunk_a[0], (g_out,), False)
    steps_a = reduce_steps(0, chunk_a)
    next(steps_a)
    pack(chunk_b[0], (g_in, g_head), True)
    steps_b = reduce_steps(1, chunk_b)
    next(steps_b)

    part_ref[blocks] = jnp.zeros((cells, channels), f32)

    def merge(i, carry):
        j = blocks - 1 - i
        row, later = rows_smem[0, 0, j], blocks
        for other in range(blocks - 1, 0, -1):
            same = (rows_smem[0, 0, other] == row) & (other > j)
            later = jnp.where(same, other, later)
        part_ref[j] = part_ref[j] + part_ref[later]
        return carry

    lax.fori_loop(0, blocks, merge, 0)
    next(steps_a)
    next(steps_b)
    for c in last_edges:
        c.wait_recv()
    edge_f[...] = 0.5 * edge_recv[2:4].astype(f32)

    def gather(r, carry):
        found = blocks
        for j in range(blocks - 1, -1, -1):
            found = jnp.where(rows_smem[0, 0, j] == r, j, found)
        lat_out[r] = part_ref[found]
        lat_out[r, 0:1, :] += edge_f[0, pl.ds(r, 1), :]
        lat_out[r, cells - 1 : cells, :] += edge_f[1, pl.ds(r, 1), :]
        return carry

    lax.fori_loop(0, lat_rows, gather, 0)
    store = pltpu.make_async_copy(lat_out, rows_out, store_sem)
    store.start()
    for _ in range(5):
        next(steps_a)
        next(steps_b)
    split = chunk_a[0].shape[0]
    sums_ref[0:split, :] = chunk_a[-1][...]
    sums_ref[split:, :] = chunk_b[-1][...]

    for copy in started + first_edges + last_edges:
        copy.wait_send()
    for m in range(1, peers):
        for copy in sends[m]:
            copy.wait_send()
    store.wait()


def layer(latent, rows, weights, slots, counts, targets, gain, w_in, w_out, head, peers, bands):
    lat_rows, cells, channels = latent.shape
    blocks, obs = slots.shape
    hid = w_in.shape[1]
    values = head.shape[1]
    vmem, anym = pl.BlockSpec(memory_space=pltpu.VMEM), pl.BlockSpec(memory_space=pl.ANY)
    smem = pl.BlockSpec(memory_space=pltpu.SMEM)
    shape = jax.ShapeDtypeStruct
    dma = pltpu.SemaphoreType.DMA
    flops = 2 * blocks * cells * channels * (6 * hid + 4 * obs + 3 * values)
    pieces, ranks = bands * peers, peers // 2

    def chunk(lines):
        total = pieces * 16 * pl.cdiv(lines, pieces * 16)
        half, quarter, piece = total // 2, total // 2 // bands, total // pieces
        shapes = [
            (total, 128),
            (half, 128),
            (half, 128),
            (bands - 1, quarter, 128),
            (quarter, 128),
            (ranks - 1, piece, 128),
            (total, 128),
        ]
        return total, tuple(pltpu.VMEM(one, bf16) for one in shapes)

    total_a, chunk_a = chunk(channels * hid // 128)
    total_b, chunk_b = chunk(channels * (hid + values) // 128 + 16)
    return pl.pallas_call(
        functools.partial(layer_kernel, peers, bands),
        out_shape=[
            shape((lat_rows, cells, channels), f32),
            shape((total_a + total_b, 128), bf16),
        ],
        in_specs=[smem] * 2 + [anym] * 8,
        out_specs=[anym, vmem],
        scratch_shapes=[
            pltpu.VMEM((blocks + 1, cells, channels), f32),
            pltpu.VMEM((lat_rows, cells, channels), f32),
            pltpu.VMEM(latent.shape, bf16),
            pltpu.VMEM((blocks, obs), jnp.int32),
            pltpu.VMEM((1, channels), f32),
            pltpu.VMEM(w_in.shape, bf16),
            pltpu.VMEM(w_out.shape, bf16),
            pltpu.VMEM(head.shape, bf16),
            pltpu.VMEM(w_in.shape, f32),
            pltpu.VMEM(w_out.shape, f32),
            pltpu.VMEM((1, channels), f32),
            pltpu.VMEM(head.shape, f32),
            pltpu.VMEM((blocks, lat_rows), f32),
            pltpu.VMEM((blocks, obs), f32),
            chunk_a,
            chunk_b,
            pltpu.VMEM((blocks, obs, cells), bf16),
            pltpu.VMEM((blocks, obs, values), bf16),
            pltpu.VMEM((blocks, 8, obs), f32),
            pltpu.VMEM((blocks, 8, obs), f32),
            pltpu.VMEM((2, lat_rows, channels), f32),
            pltpu.VMEM((4, lat_rows, channels), bf16),
            pltpu.VMEM((4, lat_rows, channels), bf16),
            pltpu.VMEM((2, blocks, channels), f32),
            pltpu.VMEM((blocks, cells, channels), f32),
            pltpu.VMEM((blocks, cells, 1), f32),
            pltpu.VMEM((blocks, cells, channels), bf16),
            pltpu.VMEM((blocks, cells, hid), bf16),
            pltpu.VMEM((blocks, cells, hid), f32),
            pltpu.VMEM((blocks, cells, channels), bf16),
            pltpu.VMEM((2, blocks, channels), f32),
        ]
        + [dma((peers,))] * 6
        + [dma((4,))] * 2
        + [dma((6,)), dma(()), dma((2, 2, 2))]
        + [dma((2, 2, 2 * (bands - 1))), dma((2, 2, 2 * (ranks - 1)))],
        compiler_params=pltpu.CompilerParams(
            collective_id=0, has_side_effects=True, vmem_limit_bytes=56 * 1024 * 1024
        ),
        cost_estimate=pl.CostEstimate(
            flops=flops, bytes_accessed=10 * 1024 * 1024, transcendentals=blocks * cells * hid
        ),
    )(
        rows,
        counts,
        latent,
        weights,
        targets,
        slots,
        gain.reshape(1, channels),
        w_in,
        w_out,
        head,
    )


def finish_kernel(
    scale, split, rows_ref, sums_hbm, out_ref, w_in_g, w_out_g, gain_g, head_g, held, sums_ref, sems
):
    count = sems.shape[1] - 1
    size = rows_ref.shape[0] // count
    load = pltpu.make_async_copy(sums_hbm, sums_ref, sems.at[0, count])
    load.start()
    reads, writes = [], []
    for i in range(count):
        part = pl.ds(i * size, size)
        reads.append(pltpu.make_async_copy(rows_ref.at[part], held.at[part], sems.at[0, i]))
        writes.append(pltpu.make_async_copy(held.at[part], out_ref.at[part], sems.at[1, i]))
        reads[-1].start()
    for i in range(count):
        reads[i].wait()
        writes[i].start()
    load.wait()
    at = 0
    for grad in (w_out_g, w_in_g, head_g):
        for lane in range(0, grad.shape[1], 128):
            part = sums_ref[at : at + grad.shape[0], :].astype(f32)
            grad[:, lane : lane + 128] = part * scale
            at += grad.shape[0]
        if grad is w_out_g:
            at = split
    lines = sums_ref[at : at + 16, :].astype(f32) * scale
    for i in range(gain_g.shape[1] // 128):
        gain_g[:, i * 128 : (i + 1) * 128] = lines[i : i + 1]
    for write in writes:
        write.wait()


def finish(rows, sums, w_in, w_out, head, scale, split):
    channels = rows.shape[2]
    vmem, anym = pl.BlockSpec(memory_space=pltpu.VMEM), pl.BlockSpec(memory_space=pl.ANY)
    shape = jax.ShapeDtypeStruct
    return pl.pallas_call(
        functools.partial(finish_kernel, scale, split),
        out_shape=[
            shape(rows.shape, f32),
            shape(w_in.shape, f32),
            shape(w_out.shape, f32),
            shape((1, channels), f32),
            shape(head.shape, f32),
        ],
        in_specs=[anym] * 2,
        out_specs=[anym] + [vmem] * 4,
        scratch_shapes=[
            pltpu.VMEM(rows.shape, f32),
            pltpu.VMEM(sums.shape, bf16),
            pltpu.SemaphoreType.DMA((2, 9)),
        ],
        compiler_params=pltpu.CompilerParams(vmem_limit_bytes=56 * 1024 * 1024),
        cost_estimate=pl.CostEstimate(
            flops=sums.size, bytes_accessed=8 * rows.size + 6 * sums.size, transcendentals=0
        ),
    )(rows, sums)


def body(latent, row_index, weights, slots, counts, targets, gain, w_in, w_out, head):
    peers, bands = lax.axis_size("lon"), lax.axis_size("band")
    split = 16 * bands * peers
    split = split * pl.cdiv(w_in.size // 128, split)
    rows, sums = layer(
        latent, row_index, weights, slots, counts, targets, gain, w_in, w_out, head, peers, bands
    )
    grad_latent, g_in, g_out, g_gain, g_head = finish(
        rows, sums, w_in, w_out, head, 1.0 / (peers * bands), split
    )
    return grad_latent, g_in, g_out, g_gain.reshape(-1), g_head


def solution(mesh):
    return jax.shard_map(
        body,
        mesh=mesh,
        in_specs=(
            P("band", "lon", None),
            P("band", "lon", None),
            P(("band", "lon"), None, None),
            P(("band", "lon"), None),
            P(("band", "lon")),
            P(("band", "lon"), None, None),
            P(),
            P(),
            P(),
            P(),
        ),
        out_specs=(P("band", "lon", None), P(), P(), P(), P()),
        check_vma=False,
    )
```

time: 79.4 us -> 61.3 us (0.77)
  Pallas kernels: 75 us -> 60.4 us
  local copies, waits for them, and re-layouts: 3.51 us -> 0 us
    pallas_call x1, Pallas kernels: 69.2 us -> 55.6 us  [layer(): pl.pallas_call(functools.partial(layer_kernel, peers, bands), out_shape=[...]
    unnamed x8 -> x0, local copies, waits for them, and re-layouts: 3.51 us -> none
    pallas_call x1, Pallas kernels: 5.83 us -> 4.8 us  [finish(): pl.pallas_call(functools.partial(finish_kernel, scale, split), out_shape=...]
where the time goes in v3:
time: 61.3 us; the launch traced here: 61 us
  Pallas kernels  60.4 us (99%)
  between operations  0.64 us (1%)
    pallas_call x1, Pallas kernels, layer(): pl.pallas_call(functools.partial(layer_kernel, peers, bands), out_shape=[...  55.6 us
    pallas_call x1, Pallas kernels, finish(): pl.pallas_call(functools.partial(finish_kernel, scale, split), out_shape=...  4.8 us

profile of v3, /device:TPU:0, one launch (start us, length us, event | category | flops | bytes accessed | tf_op | source)
XLA Modules:
  0.0 61.0 jit_solution(18406060699017895582)
XLA Ops:
  0.6 55.6 %shard_map.137 = (f32[32,128,256]{2,1,0:T(8,128)}, bf16[2560,128]{1,0:T(8,128)(2,1)}) custom-call(s32[1,1,16]{2,1,0:T(1,128)} %rows_smem.1, s32[16]{0:T(128)} %count_smem.1, bf16[32,128,256]{2,1,0:T(8,128)(2,1)} %lat_hbm.1, bf16[16,128,128]{2,1,0:T(8,128)(2,1)} %w_ref.1, bf16[16,128,128]{2,1,0:T(8,128)(2,1)} %t_ref.1, s32[16,128]{1,0:T(8,128)} %slot_hbm.1, ...), custom_call_target="tpu_custom_call" | custom-call | flops 4160749568 | bytes 10485760 | tf_op jit(solution)/shard_map/pallas_call | solution.py:495
  56.2 4.8 %shard_map.138 = (f32[32,128,256]{2,1,0:T(8,128)}, f32[256,512]{1,0:T(8,128)}, f32[512,256]{1,0:T(8,128)}, f32[1,256]{1,0:T(1,128)}, f32[256,128]{1,0:T(8,128)}) custom-call(f32[32,128,256]{2,1,0:T(8,128)} %get-tuple-element.12.rows_ref, bf16[2560,128]{1,0:T(8,128)(2,1)} %get-tuple-element.13.sums_hbm), custom_call_target="tpu_custom_call" | custom-call | flops 327680 | bytes 10354688 | tf_op jit(solution)/shard_map/pallas_call | solution.py:596

commit v4 on v3

--- a/solution.py
+++ b/solution.py
@@ -75,7 +75,7 @@
     normed_s,
     act_s,
     slope_s,
-    adv_s,
+    pair_s,
     sg_edge,
     send_w,
     send_t,
@@ -189,13 +189,17 @@
     pltpu.make_async_copy(aux.at[mine], auxbuf.at[mine], recv_a.at[me]).start()
     pltpu.make_async_copy(w_ref.at[mine], wbuf.at[mine], recv_w.at[me]).start()
     pltpu.make_async_copy(t_ref.at[mine], tbuf.at[mine], recv_t.at[me]).start()
-    far = list(range(peers // 2, peers - 1))
+
+    def launch(waves):
+        for m in waves:
+            sends[m][1].start()
+            sends[m][2].start()
+
+    far = list(range(peers // 2, peers - 2))
     order = [1]
     for m in range(2, peers // 2):
         order += [far.pop(0), m]
-    for m in order + far:
-        sends[m][1].start()
-        sends[m][2].start()
+    launch(order + far)
 
     g_in[...] = jnp.zeros_like(g_in)
     g_out[...] = jnp.zeros_like(g_out)
@@ -211,7 +215,8 @@
     sel[0] = dot(onehot, edge_recv[0])
     sel[1] = dot(onehot, edge_recv[1])
 
-    group = 2 * per if blocks % (2 * per) == 0 else per
+    group = 2 * per
+    groups = blocks // group
 
     def forward(i, carry):
         xs, normeds = [], []
@@ -224,22 +229,28 @@
             normed = (u * gain).astype(bf16)
             u_s[j] = u
             inv_s[j] = inv
-            normed_s[j] = normed
             xs.append(x)
             normeds.append(normed)
-        pre = dot(jnp.concatenate(normeds, axis=0), w_in_ref[...])
+        normed = jnp.concatenate(normeds, axis=0)
+        normed_s[i] = normed.T
+        pre = dot(normed, w_in_ref[...])
         sig = jax.nn.sigmoid(pre)
         act = (pre * sig).astype(bf16)
-        slope = sig * (1.0 + pre * (1.0 - sig))
+        act_s[i] = act.T
+        slope_s[i] = sig * (1.0 + pre * (1.0 - sig))
         adv = (jnp.concatenate(xs, axis=0) + dot(act, w_out_ref[...])).astype(bf16)
         for k in range(group):
             j, sl = i * group + k, slice(k * cells, (k + 1) * cells)
-            act_s[j] = act[sl]
-            slope_s[j] = slope[sl]
-            adv_s[j] = adv[sl]
+            pair_s[j, :, 0:channels] = xs[k].astype(bf16)
+            pair_s[j, :, channels:] = adv[sl]
+
+        @pl.when(i == groups - 2)
+        def _():
+            launch([peers - 2])
+
         return carry
 
-    lax.fori_loop(0, blocks // group, forward, 0)
+    lax.fori_loop(0, groups, forward, 0)
 
     eye = lax.broadcasted_iota(jnp.int32, (obs, obs), 0) == lax.broadcasted_iota(
         jnp.int32, (obs, obs), 1
@@ -247,62 +258,56 @@
     loss_scale = 1.0 / math.sqrt(obs)
 
     def backward(i, carry):
-        s, bit = me, 1
-        while bit < peers:
-            s = s + lax.rem(i // bit, 2) * bit * (1 - 2 * ((me // bit) % 2))
+        chip, bit = me // 2, 1
+        while bit < groups:
+            chip = chip + lax.rem(i // bit, 2) * bit * (1 - 2 * ((me // 2 // bit) % 2))
             bit *= 2
 
-        @pl.when(i == peers // 2 - 2)
+        @pl.when(i == groups // 2 - 1)
         def _():
-            sends[peers - 1][1].start()
-            sends[peers - 1][2].start()
-
-        base = s * per
-        span = pl.ds(base, per)
-        for buf, sem in ((wbuf, recv_w), (tbuf, recv_t), (auxbuf, recv_a)):
-            pltpu.make_async_copy(buf.at[span], buf.at[span], sem.at[s]).wait()
+            launch([peers - 1])
+
+        base = chip * group
+        span = pl.ds(base, group)
+        for s in (2 * chip, 2 * chip + 1):
+            part = pl.ds(s * per, per)
+            for buf, sem in ((wbuf, recv_w), (tbuf, recv_t), (auxbuf, recv_a)):
+                pltpu.make_async_copy(buf.at[part], buf.at[part], sem.at[s]).wait()
         codes, lats = [], []
-        for k in range(per):
+        for k in range(group):
             code = jnp.where(eye, auxbuf[base + k][0:1, :], 0.0)
             code = jnp.sum(code, axis=1, keepdims=True)
             codes.append(code)
             c = jnp.maximum(code, 0.0)
-            w = wbuf[base + k]
-            old = dot(w, lat_ref[rows_smem[0, 0, base + k]])
-            new = dot(w, adv_s[base + k])
-            lats.append(((1.0 - c) * old + c * new).astype(bf16))
+            both = dot(wbuf[base + k], pair_s[base + k])
+            lats.append(((1.0 - c) * both[:, :channels] + c * both[:, channels:]).astype(bf16))
         obs_latent = jnp.concatenate(lats, axis=0)
         code = jnp.concatenate(codes, axis=0)
         c = jnp.maximum(code, 0.0)
         head = head_ref[...]
         predicted = dot(obs_latent, head)
-        goals = tbuf[span].reshape(per * obs, head.shape[1]).astype(f32)
+        goals = tbuf[span].reshape(group * obs, head.shape[1]).astype(f32)
         residual = jnp.where(code >= 0.0, predicted - goals, 0.0)
         pred_grad = (residual * loss_scale).astype(bf16)
         g_head[...] += dot(obs_latent, pred_grad, TN)
         obs_grad = dot(pred_grad, head, NT).astype(bf16).astype(f32)
-        back_old = ((1.0 - c) * obs_grad).astype(bf16)
-        back_new = (c * obs_grad).astype(bf16)
+        back = jnp.concatenate([(1.0 - c) * obs_grad, c * obs_grad], axis=1).astype(bf16)
         olds, news = [], []
-        for k in range(per):
-            w = wbuf[base + k]
-            sl = slice(k * obs, (k + 1) * obs)
-            olds.append(dot(w, back_old[sl], TN).astype(bf16))
-            news.append(dot(w, back_new[sl], TN).astype(bf16))
+        for k in range(group):
+            both = dot(wbuf[base + k], back[k * obs : (k + 1) * obs], TN).astype(bf16)
+            olds.append(both[:, :channels])
+            news.append(both[:, channels:])
         tile_new = jnp.concatenate(news, axis=0)
-        act = act_s[span].reshape(per * cells, -1)
-        slope = slope_s[span].reshape(per * cells, -1)
-        normed = normed_s[span].reshape(per * cells, channels)
-        u = u_s[span].reshape(per * cells, channels)
-        g_out[...] += dot(act, tile_new, TN)
-        pre_grad = (dot(tile_new, w_out_ref[...], NT) * slope).astype(bf16)
-        g_in[...] += dot(normed, pre_grad, TN)
+        u = u_s[span].reshape(group * cells, channels)
+        g_out[...] += dot(act_s[chip], tile_new)
+        pre_grad = (dot(tile_new, w_out_ref[...], NT) * slope_s[chip]).astype(bf16)
+        g_in[...] += dot(normed_s[chip], pre_grad)
         normed_grad = dot(pre_grad, w_in_ref[...], NT)
         ng_u = normed_grad * u
         g_gain[...] += jnp.sum(ng_u, axis=0, keepdims=True)
         mean = jnp.mean(ng_u * gain, axis=-1, keepdims=True)
         core = normed_grad * gain - u * mean
-        for k in range(per):
+        for k in range(group):
             sl = slice(k * cells, (k + 1) * cells)
             sg = inv_s[base + k] * core[sl]
             sg_edge[0, pl.ds(base + k, 1), :] = sg[cells - 1 : cells]
@@ -312,7 +317,7 @@
             )
         return carry
 
-    lax.fori_loop(0, peers, backward, 0)
+    lax.fori_loop(0, groups, backward, 0)
 
     edge_send[2] = dot(onehot, sg_edge[0].astype(bf16), TN).astype(bf16)
     edge_send[3] = dot(onehot, sg_edge[1].astype(bf16), TN).astype(bf16)
@@ -447,21 +452,26 @@
         return carry
 
     lax.fori_loop(0, lat_rows, gather, 0)
-    store = pltpu.make_async_copy(lat_out, rows_out, store_sem)
+    store = pltpu.make_async_copy(lat_out, rows_out, store_sem.at[0])
     store.start()
     for _ in range(5):
         next(steps_a)
         next(steps_b)
     split = chunk_a[0].shape[0]
-    sums_ref[0:split, :] = chunk_a[-1][...]
-    sums_ref[split:, :] = chunk_b[-1][...]
+    stores = [
+        pltpu.make_async_copy(chunk_a[-1], sums_ref.at[0:split], store_sem.at[1]),
+        pltpu.make_async_copy(chunk_b[-1], sums_ref.at[split:], store_sem.at[2]),
+    ]
+    for copy in stores:
+        copy.start()
 
     for copy in started + first_edges + last_edges:
         copy.wait_send()
     for m in range(1, peers):
         for copy in sends[m]:
             copy.wait_send()
-    store.wait()
+    for copy in [store] + stores:
+        copy.wait()
 
 
 def layer(latent, rows, weights, slots, counts, targets, gain, w_in, w_out, head, peers, bands):
@@ -499,7 +509,7 @@
             shape((total_a + total_b, 128), bf16),
         ],
         in_specs=[smem] * 2 + [anym] * 8,
-        out_specs=[anym, vmem],
+        out_specs=[anym, anym],
         scratch_shapes=[
             pltpu.VMEM((blocks + 1, cells, channels), f32),
             pltpu.VMEM((lat_rows, cells, channels), f32),
@@ -527,15 +537,15 @@
             pltpu.VMEM((2, blocks, channels), f32),
             pltpu.VMEM((blocks, cells, channels), f32),
             pltpu.VMEM((blocks, cells, 1), f32),
-            pltpu.VMEM((blocks, cells, channels), bf16),
-            pltpu.VMEM((blocks, cells, hid), bf16),
-            pltpu.VMEM((blocks, cells, hid), f32),
-            pltpu.VMEM((blocks, cells, channels), bf16),
+            pltpu.VMEM((ranks, channels, blocks * cells // ranks), bf16),
+            pltpu.VMEM((ranks, hid, blocks * cells // ranks), bf16),
+            pltpu.VMEM((ranks, blocks * cells // ranks, hid), f32),
+            pltpu.VMEM((blocks, cells, 2 * channels), bf16),
             pltpu.VMEM((2, blocks, channels), f32),
         ]
         + [dma((peers,))] * 6
         + [dma((4,))] * 2
-        + [dma((6,)), dma(()), dma((2, 2, 2))]
+        + [dma((6,)), dma((3,)), dma((2, 2, 2))]
         + [dma((2, 2, 2 * (bands - 1))), dma((2, 2, 2 * (ranks - 1)))],
         compiler_params=pltpu.CompilerParams(
             collective_id=0, has_side_effects=True, vmem_limit_bytes=56 * 1024 * 1024

time: 61.3 us -> 61.5 us (level); the launches traced: 61 us -> 60.5 us
  no operation moved by 1% of the time
where the time goes in v4:
time: 61.5 us; the launch traced here: 60.5 us
  Pallas kernels  59.9 us (97%)
  between operations  0.64 us (1%)
    pallas_call x1, Pallas kernels, layer(): pl.pallas_call(functools.partial(layer_kernel, peers, bands), out_shape=[...  55.1 us
    pallas_call x1, Pallas kernels, finish(): pl.pallas_call(functools.partial(finish_kernel, scale, split), out_shape=...  4.8 us

profile of v4, /device:TPU:0, one launch (start us, length us, event | category | flops | bytes accessed | tf_op | source)
XLA Modules:
  0.0 60.5 jit_solution(4065555017840126378)
XLA Ops:
  0.6 55.1 %shard_map.137 = (f32[32,128,256]{2,1,0:T(8,128)}, bf16[2560,128]{1,0:T(8,128)(2,1)}) custom-call(s32[1,1,16]{2,1,0:T(1,128)} %rows_smem.1, s32[16]{0:T(128)} %count_smem.1, bf16[32,128,256]{2,1,0:T(8,128)(2,1)} %lat_hbm.1, bf16[16,128,128]{2,1,0:T(8,128)(2,1)} %w_ref.1, bf16[16,128,128]{2,1,0:T(8,128)(2,1)} %t_ref.1, s32[16,128]{1,0:T(8,128)} %slot_hbm.1, ...), custom_call_target="tpu_custom_call" | custom-call | flops 4160749568 | bytes 10485760 | tf_op jit(solution)/shard_map/pallas_call | solution.py:505
  55.7 4.8 %shard_map.138 = (f32[32,128,256]{2,1,0:T(8,128)}, f32[256,512]{1,0:T(8,128)}, f32[512,256]{1,0:T(8,128)}, f32[1,256]{1,0:T(1,128)}, f32[256,128]{1,0:T(8,128)}) custom-call(f32[32,128,256]{2,1,0:T(8,128)} %get-tuple-element.12.rows_ref, bf16[2560,128]{1,0:T(8,128)(2,1)} %get-tuple-element.13.sums_hbm), custom_call_target="tpu_custom_call" | custom-call | flops 327680 | bytes 10354688 | tf_op jit(solution)/shard_map/pallas_call | solution.py:606

commit v5 on v4

--- a/solution.py
+++ b/solution.py
@@ -122,21 +122,6 @@
     for load in loads:
         load.start()
 
-    lane = lax.broadcasted_iota(jnp.int32, (1, obs), 1)
-    row_lane = lax.broadcasted_iota(jnp.int32, (1, lat_rows), 1)
-    for j in range(blocks):
-        live_f[j : j + 1, :] = (lane < count_smem[j]).astype(f32)
-        onehot_f[j : j + 1, :] = (row_lane == rows_smem[0, 0, j]).astype(f32)
-    loads[0].wait()
-    coef = (slot_ref[...].astype(f32) / (WINDOW_SLOTS - 1)).astype(bf16).astype(f32)
-    coded = jnp.where(live_f[...] > 0.0, coef, -1.0)
-    aux[...] = jnp.broadcast_to(coded[:, None, :], aux.shape)
-    loads[1].wait()
-    for r in range(lat_rows):
-        edge_f[0, r : r + 1, :] = lat_ref[r, cells - 16 : cells, :].astype(f32)[15:16]
-        edge_f[1, r : r + 1, :] = lat_ref[r, 0:16, :].astype(f32)[0:1]
-    edge_send[0:2] = edge_f[...].astype(bf16)
-
     barrier = pltpu.get_barrier_semaphore()
     for d in range(1, peers):
         pl.semaphore_signal(
@@ -148,28 +133,13 @@
         )
     pl.semaphore_wait(barrier, peers + bands - 2)
 
-    def edge_copy(phase, side):
-        slot = 2 * phase + side
-        return pltpu.make_async_remote_copy(
-            src_ref=edge_send.at[slot],
-            dst_ref=edge_recv.at[slot],
-            send_sem=send_e.at[slot],
-            recv_sem=recv_e.at[slot],
-            device_id={"lon": left if side else right},
-            device_id_type=MESH,
-        )
-
-    first_edges = [edge_copy(0, 0), edge_copy(0, 1)]
-    for c in first_edges:
-        c.start()
-
     def exchange(m):
         to = partner(m)
         src, dst = pl.ds(to * per, per), pl.ds(me * per, per)
         return [
             pltpu.make_async_remote_copy(
-                src_ref=a.at[src],
-                dst_ref=b.at[dst],
+                src_ref=a.at[to if a is aux else src],
+                dst_ref=b.at[me if a is aux else dst],
                 send_sem=ss.at[to],
                 recv_sem=rs.at[me],
                 device_id={"lon": to},
@@ -183,23 +153,56 @@
         ]
 
     sends = [None] + [exchange(m) for m in range(1, peers)]
-    for m in range(1, peers):
-        sends[m][0].start()
     mine = pl.ds(me * per, per)
-    pltpu.make_async_copy(aux.at[mine], auxbuf.at[mine], recv_a.at[me]).start()
-    pltpu.make_async_copy(w_ref.at[mine], wbuf.at[mine], recv_w.at[me]).start()
-    pltpu.make_async_copy(t_ref.at[mine], tbuf.at[mine], recv_t.at[me]).start()
 
     def launch(waves):
         for m in waves:
             sends[m][1].start()
             sends[m][2].start()
 
-    far = list(range(peers // 2, peers - 2))
-    order = [1]
+    launch([peers // 2, 1])
+    pltpu.make_async_copy(w_ref.at[mine], wbuf.at[mine], recv_w.at[me]).start()
+    pltpu.make_async_copy(t_ref.at[mine], tbuf.at[mine], recv_t.at[me]).start()
+
+    lane = lax.broadcasted_iota(jnp.int32, (1, obs), 1)
+    row_lane = lax.broadcasted_iota(jnp.int32, (1, lat_rows), 1)
+    for j in range(blocks):
+        live_f[j : j + 1, :] = (lane < count_smem[j]).astype(f32)
+        onehot_f[j : j + 1, :] = (row_lane == rows_smem[0, 0, j]).astype(f32)
+    loads[0].wait()
+    coef = (slot_ref[...].astype(f32) / (WINDOW_SLOTS - 1)).astype(bf16).astype(f32)
+    coded = jnp.where(live_f[...] > 0.0, coef, -1.0)
+    aux[...] = jnp.zeros_like(aux)
+    for p in range(peers):
+        aux[p, 0:per, :] = coded[p * per : (p + 1) * per]
+    loads[1].wait()
+    for r in range(lat_rows):
+        edge_f[0, r : r + 1, :] = lat_ref[r, cells - 16 : cells, :].astype(f32)[15:16]
+        edge_f[1, r : r + 1, :] = lat_ref[r, 0:16, :].astype(f32)[0:1]
+    edge_send[0:2] = edge_f[...].astype(bf16)
+
+    def edge_copy(phase, side):
+        slot = 2 * phase + side
+        return pltpu.make_async_remote_copy(
+            src_ref=edge_send.at[slot],
+            dst_ref=edge_recv.at[slot],
+            send_sem=send_e.at[slot],
+            recv_sem=recv_e.at[slot],
+            device_id={"lon": left if side else right},
+            device_id_type=MESH,
+        )
+
+    first_edges = [edge_copy(0, 0), edge_copy(0, 1)]
+    for c in first_edges:
+        c.start()
+
+    for m in range(1, peers):
+        sends[m][0].start()
+    pltpu.make_async_copy(aux.at[me], auxbuf.at[me], recv_a.at[me]).start()
+    order = []
     for m in range(2, peers // 2):
-        order += [far.pop(0), m]
-    launch(order + far)
+        order += [m + peers // 2 - 1, m]
+    launch(order)
 
     g_in[...] = jnp.zeros_like(g_in)
     g_out[...] = jnp.zeros_like(g_out)
@@ -244,9 +247,9 @@
             pair_s[j, :, 0:channels] = xs[k].astype(bf16)
             pair_s[j, :, channels:] = adv[sl]
 
-        @pl.when(i == groups - 2)
+        @pl.when(i == groups - 1)
         def _():
-            launch([peers - 2])
+            launch([peers - 1])
 
         return carry
 
@@ -263,19 +266,16 @@
             chip = chip + lax.rem(i // bit, 2) * bit * (1 - 2 * ((me // 2 // bit) % 2))
             bit *= 2
 
-        @pl.when(i == groups // 2 - 1)
-        def _():
-            launch([peers - 1])
-
         base = chip * group
         span = pl.ds(base, group)
         for s in (2 * chip, 2 * chip + 1):
             part = pl.ds(s * per, per)
-            for buf, sem in ((wbuf, recv_w), (tbuf, recv_t), (auxbuf, recv_a)):
+            for buf, sem in ((wbuf, recv_w), (tbuf, recv_t)):
                 pltpu.make_async_copy(buf.at[part], buf.at[part], sem.at[s]).wait()
+            pltpu.make_async_copy(auxbuf.at[s], auxbuf.at[s], recv_a.at[s]).wait()
         codes, lats = [], []
         for k in range(group):
-            code = jnp.where(eye, auxbuf[base + k][0:1, :], 0.0)
+            code = jnp.where(eye, auxbuf[2 * chip + k // per][k % per : k % per + 1, :], 0.0)
             code = jnp.sum(code, axis=1, keepdims=True)
             codes.append(code)
             c = jnp.maximum(code, 0.0)
@@ -477,9 +477,10 @@
 def layer(latent, rows, weights, slots, counts, targets, gain, w_in, w_out, head, peers, bands):
     lat_rows, cells, channels = latent.shape
     blocks, obs = slots.shape
+    per = blocks // peers
     hid = w_in.shape[1]
     values = head.shape[1]
-    vmem, anym = pl.BlockSpec(memory_space=pltpu.VMEM), pl.BlockSpec(memory_space=pl.ANY)
+    anym = pl.BlockSpec(memory_space=pl.ANY)
     smem = pl.BlockSpec(memory_space=pltpu.SMEM)
     shape = jax.ShapeDtypeStruct
     dma = pltpu.SemaphoreType.DMA
@@ -529,8 +530,8 @@
             chunk_b,
             pltpu.VMEM((blocks, obs, cells), bf16),
             pltpu.VMEM((blocks, obs, values), bf16),
-            pltpu.VMEM((blocks, 8, obs), f32),
-            pltpu.VMEM((blocks, 8, obs), f32),
+            pltpu.VMEM((peers, 8 * pl.cdiv(per, 8), obs), f32),
+            pltpu.VMEM((peers, 8 * pl.cdiv(per, 8), obs), f32),
             pltpu.VMEM((2, lat_rows, channels), f32),
             pltpu.VMEM((4, lat_rows, channels), bf16),
             pltpu.VMEM((4, lat_rows, channels), bf16),
@@ -568,7 +569,23 @@
 
 
 def finish_kernel(
-    scale, split, rows_ref, sums_hbm, out_ref, w_in_g, w_out_g, gain_g, head_g, held, sums_ref, sems
+    scale,
+    split,
+    rows_ref,
+    sums_hbm,
+    out_ref,
+    w_in_hbm,
+    w_out_hbm,
+    gain_hbm,
+    head_hbm,
+    w_in_g,
+    w_out_g,
+    gain_g,
+    head_g,
+    held,
+    sums_ref,
+    sems,
+    grad_sems,
 ):
     count = sems.shape[1] - 1
     size = rows_ref.shape[0] // count
@@ -595,13 +612,17 @@
     lines = sums_ref[at : at + 16, :].astype(f32) * scale
     for i in range(gain_g.shape[1] // 128):
         gain_g[:, i * 128 : (i + 1) * 128] = lines[i : i + 1]
+    pairs = ((w_in_g, w_in_hbm), (w_out_g, w_out_hbm), (gain_g, gain_hbm), (head_g, head_hbm))
+    for i, (a, b) in enumerate(pairs):
+        writes.append(pltpu.make_async_copy(a, b, grad_sems.at[i]))
+        writes[-1].start()
     for write in writes:
         write.wait()
 
 
 def finish(rows, sums, w_in, w_out, head, scale, split):
     channels = rows.shape[2]
-    vmem, anym = pl.BlockSpec(memory_space=pltpu.VMEM), pl.BlockSpec(memory_space=pl.ANY)
+    anym = pl.BlockSpec(memory_space=pl.ANY)
     shape = jax.ShapeDtypeStruct
     return pl.pallas_call(
         functools.partial(finish_kernel, scale, split),
@@ -613,11 +634,16 @@
             shape(head.shape, f32),
         ],
         in_specs=[anym] * 2,
-        out_specs=[anym] + [vmem] * 4,
+        out_specs=[anym] * 5,
         scratch_shapes=[
+            pltpu.VMEM(w_in.shape, f32),
+            pltpu.VMEM(w_out.shape, f32),
+            pltpu.VMEM((1, channels), f32),
+            pltpu.VMEM(head.shape, f32),
             pltpu.VMEM(rows.shape, f32),
             pltpu.VMEM(sums.shape, bf16),
             pltpu.SemaphoreType.DMA((2, 9)),
+            pltpu.SemaphoreType.DMA((4,)),
         ],
         compiler_params=pltpu.CompilerParams(vmem_limit_bytes=56 * 1024 * 1024),
         cost_estimate=pl.CostEstimate(

time: 61.5 us -> 58.7 us (0.954)
  Pallas kernels: 59.9 us -> 57.2 us
    pallas_call x1, Pallas kernels: 55.1 us -> 53 us  [layer(): pl.pallas_call(functools.partial(layer_kernel, peers, bands), out_shape=[...]
    pallas_call x1, Pallas kernels: 4.8 us -> 4.18 us  [finish(): pl.pallas_call(functools.partial(finish_kernel, scale, split), out_shape=...]
where the time goes in v5:
time: 58.7 us; the launch traced here: 57.8 us
  Pallas kernels  57.2 us (97%)
  between operations  0.64 us (1%)
    pallas_call x1, Pallas kernels, layer(): pl.pallas_call(functools.partial(layer_kernel, peers, bands), out_shape=[...  53 us
    pallas_call x1, Pallas kernels, finish(): pl.pallas_call(functools.partial(finish_kernel, scale, split), out_shape=...  4.18 us

profile of v5, /device:TPU:0, one launch (start us, length us, event | category | flops | bytes accessed | tf_op | source)
XLA Modules:
  0.0 57.8 jit_solution(1438289820119400013)
XLA Ops:
  0.6 53.0 %shard_map.137 = (f32[32,128,256]{2,1,0:T(8,128)}, bf16[2560,128]{1,0:T(8,128)(2,1)}) custom-call(s32[1,1,16]{2,1,0:T(1,128)} %rows_smem.1, s32[16]{0:T(128)} %count_smem.1, bf16[32,128,256]{2,1,0:T(8,128)(2,1)} %lat_hbm.1, bf16[16,128,128]{2,1,0:T(8,128)(2,1)} %w_ref.1, bf16[16,128,128]{2,1,0:T(8,128)(2,1)} %t_ref.1, s32[16,128]{1,0:T(8,128)} %slot_hbm.1, ...), custom_call_target="tpu_custom_call" | custom-call | flops 4160749568 | bytes 10485760 | tf_op jit(solution)/shard_map/pallas_call | solution.py:506
  53.6 4.2 %shard_map.138 = (f32[32,128,256]{2,1,0:T(8,128)}, f32[256,512]{1,0:T(8,128)}, f32[512,256]{1,0:T(8,128)}, f32[1,256]{1,0:T(1,128)}, f32[256,128]{1,0:T(8,128)}) custom-call(f32[32,128,256]{2,1,0:T(8,128)} %get-tuple-element.12.rows_ref, bf16[2560,128]{1,0:T(8,128)(2,1)} %get-tuple-element.13.sums_hbm), custom_call_target="tpu_custom_call" | custom-call | flops 327680 | bytes 10354688 | tf_op jit(solution)/shard_map/pallas_call | solution.py:627
